TPU v7x, 32 devices: a whole 2x2x4 slice. The times are simulated.
32 devices in a mesh: groups: 2 (over y), inner: 4 (over z), outer: 2 (over x), heads: 2 (over core).
Axes of the slice: x: 2, y: 2, z: 4, core: 2. Of those that a mesh axis runs over, the one named last changes fastest.
Arguments:
- queries: bfloat16 [2048, 64, 128], P(('groups', 'inner'), ('outer', 'heads')), parts along dimension 0, may hold values from -6 to 6
- keys: bfloat16 [2048, 8, 128], P(('groups', 'inner')), parts along dimension 0, may hold values from -6 to 6
- values: bfloat16 [2048, 8, 128], P(('groups', 'inner')), parts along dimension 0, may hold values from -6 to 6
- grad_out: bfloat16 [2048, 64, 128], P(('groups', 'inner'), ('outer', 'heads')), parts along dimension 0, may hold values from -6 to 6
- seg_ids: int32 [2048], P(('groups', 'inner')), parts along dimension 0, may hold values from 0 to 3, never falling along the last dimension, each value on 1 to 512 neighbouring positions
Outputs:
- attn_out: bfloat16 [2048, 64, 128], P(('groups', 'inner'), ('outer', 'heads')), parts along dimension 0
- grad_q: bfloat16 [2048, 64, 128], P(('groups', 'inner'), ('outer', 'heads')), parts along dimension 0
- grad_k: bfloat16 [2048, 8, 128], P(('groups', 'inner')), parts along dimension 0
- grad_v: bfloat16 [2048, 8, 128], P(('groups', 'inner')), parts along dimension 0
There are 2 independent parts, one for each index of `groups`. A program takes and returns all parts, laid end to end along the dimension named above; each array names one. Nothing has to cross between parts.
Inputs may be any that keep to these rules, and one draw needn't show every extreme that they name: `seg_ids`: trajectory numbers never fall along the sequence; each trajectory holds 1 to 512 consecutive tokens, and one holds exactly 512.
All inputs are finite; a program needn't handle non-finite values.
Results may differ from a plain program's by a relative error of at most 0.0073.
Values may be sent and summed in bfloat16 or wider, within the bound.
A program may use at most 64 MiB of HBM per device.

v0:
```python
from functools import reduce

import jax
import jax.numpy as jnp
from jax import lax
from jax.sharding import PartitionSpec as P

GROUP = 8


masked_score = -1e30


def passed_along(array, axis, by):
    size = lax.axis_size(axis)
    pairs = [(i, i + by) for i in range(size) if 0 <= i + by < size]
    return lax.ppermute(array, axis, pairs)


def passed_along_2(block, axis, distance):
    devices = range(lax.axis_size(axis))
    route = [((i - distance) % len(devices), i) for i in devices]
    return lax.ppermute(block, axis, route)


def shards(queries, keys, values, grad_out, seg_ids):
    tok_rows = queries.shape[0]
    heads_local = queries.shape[1]
    head_depth = queries.shape[2]
    kv_total = keys.shape[1]
    group_here = min(GROUP, heads_local)
    kv_local = heads_local // group_here
    reach_count = lax.axis_size("inner") // 2
    softmax_scale = head_depth ** (-0.5)
    head_index = lax.axis_index(("outer", "heads"))
    kv_slot = head_index * heads_local // GROUP
    key_own = lax.dynamic_slice_in_dim(keys, kv_slot, kv_local, 1)
    value_own = lax.dynamic_slice_in_dim(values, kv_slot, kv_local, 1)
    position = lax.axis_index("inner")
    segs_all = lax.all_gather(seg_ids, "inner", axis=0, tiled=True)
    row_offsets = jnp.arange(tok_rows, dtype=jnp.int32)
    query_pos = position * tok_rows + row_offsets
    q_grouped = queries.reshape(tok_rows, kv_local, group_here, head_depth)
    grad_grouped = grad_out.reshape(tok_rows, kv_local, group_here, head_depth)

    def allowed_for(distance):
        source = position - distance
        key_seg = lax.dynamic_slice_in_dim(segs_all, jnp.maximum(source, 0) * tok_rows, tok_rows, 0)
        key_pos = source * tok_rows + row_offsets
        return (
            (source >= 0)
            & (key_pos[None, :] <= query_pos[:, None])
            & (key_seg[None, :] == seg_ids[:, None])
        )

    received = [(key_own, value_own)]
    holding = (key_own, value_own)
    for distance in range(reach_count):
        holding = passed_along((holding[0], holding[1]), "inner", 1)
        received.append(holding)
    allowed_list = [allowed_for(distance) for distance in range(reach_count + 1)]
    score_list = []
    for distance in range(reach_count + 1):
        raw_scores = (
            jnp.einsum(
                "tgjd,wgd->gjtw",
                q_grouped,
                received[distance][0],
                preferred_element_type=jnp.float32,
            )
            * softmax_scale
        )
        score_list.append(jnp.where(allowed_list[distance][None, None], raw_scores, masked_score))
    row_max = reduce(jnp.maximum, [jnp.max(block, -1) for block in score_list])
    row_total = reduce(
        jnp.add, [jnp.sum(jnp.exp(block - row_max[..., None]), -1) for block in score_list]
    )
    log_total = row_max + jnp.log(row_total)
    out_acc = jnp.zeros((tok_rows, kv_local, group_here, head_depth), jnp.float32)
    for distance in range(reach_count + 1):
        weights = jnp.exp(score_list[distance] - log_total[..., None]).astype(jnp.bfloat16)
        out_acc = out_acc + jnp.einsum(
            "gjtw,wgd->tgjd", weights, received[distance][1], preferred_element_type=jnp.float32
        )
    attn_out = out_acc.reshape(tok_rows, heads_local, head_depth).astype(jnp.bfloat16)
    row_delta = jnp.sum(grad_out.astype(jnp.float32) * attn_out.astype(jnp.float32), -1)
    row_delta = row_delta.reshape(tok_rows, kv_local, group_here).transpose(1, 2, 0)
    query_grad = jnp.zeros((tok_rows, kv_local, group_here, head_depth), jnp.float32)
    zero_grads = jnp.zeros((tok_rows, kv_local, head_depth), jnp.float32)
    grad_acc = (zero_grads, zero_grads)
    holding = (key_own, value_own)
    for distance in range(reach_count + 1):
        if distance > 0:
            holding = passed_along((holding[0], holding[1]), "inner", 1)
            grad_acc = passed_along_2((grad_acc[0], grad_acc[1]), "inner", 1)
        key_block = holding[0]
        value_block = holding[1]
        probs_full = jnp.exp(score_list[distance] - log_total[..., None])
        compute_weights = probs_full.astype(jnp.bfloat16)
        grad_probs = jnp.einsum(
            "tgjd,wgd->gjtw", grad_grouped, value_block, preferred_element_type=jnp.float32
        )
        grad_scores = (softmax_scale * probs_full * (grad_probs - row_delta[..., None])).astype(
            jnp.bfloat16
        )
        query_term = jnp.einsum(
            "gjtw,wgd->tgjd", grad_scores, key_block, preferred_element_type=jnp.float32
        )
        key_term = jnp.einsum(
            "gjtw,tgjd->wgd", grad_scores, q_grouped, preferred_element_type=jnp.float32
        )
        value_term = jnp.einsum(
            "gjtw,tgjd->wgd", compute_weights, grad_grouped, preferred_element_type=jnp.float32
        )
        query_term, key_term, value_term = (query_term, key_term, value_term)
        query_grad = query_grad + query_term
        grad_acc = (grad_acc[0] + key_term, grad_acc[1] + value_term)
    grad_acc = (
        passed_along_2(grad_acc[0].astype(jnp.bfloat16), "inner", -reach_count).astype(jnp.float32),
        passed_along_2(grad_acc[1].astype(jnp.bfloat16), "inner", -reach_count).astype(jnp.float32),
    )
    empty_full = jnp.zeros((tok_rows, kv_total, head_depth), jnp.float32)
    key_placed = lax.dynamic_update_slice_in_dim(empty_full, grad_acc[0], kv_slot, 1)
    value_placed = lax.dynamic_update_slice_in_dim(empty_full, grad_acc[1], kv_slot, 1)
    key_total, value_total = (
        lax.psum(key_placed.astype(jnp.bfloat16), ("outer", "heads")).astype(jnp.float32),
        lax.psum(value_placed.astype(jnp.bfloat16), ("outer", "heads")).astype(jnp.float32),
    )
    grad_q = query_grad.reshape(tok_rows, heads_local, head_depth).astype(jnp.bfloat16)
    return (attn_out, grad_q, key_total.astype(jnp.bfloat16), value_total.astype(jnp.bfloat16))


def solution(mesh):
    return jax.shard_map(
        shards,
        mesh=mesh,
        in_specs=(
            P(("groups", "inner"), ("outer", "heads"), None),
            P(("groups", "inner"), None, None),
            P(("groups", "inner"), None, None),
            P(("groups", "inner"), ("outer", "heads"), None),
            P(("groups", "inner")),
        ),
        out_specs=(
            P(("groups", "inner"), ("outer", "heads"), None),
            P(("groups", "inner"), ("outer", "heads"), None),
            P(("groups", "inner"), None, None),
            P(("groups", "inner"), None, None),
        ),
        check_vma=False,
    )
```

profile of v0, /device:TPU:1, one launch (start us, length us, event | category | flops | bytes accessed | tf_op | source)
XLA Modules:
  0.0 145.4 jit_solution(5842437525400108166)
XLA Ops:
  7.2 1.3 constant_dynamic-slice_fusion
  8.5 4.0 %collective-permute-start = (bf16[256,2,128]{2,0,1:T(8,128)(2,1)S(1)}, bf16[256,2,128]{2,0,1:T(8,128)(2,1)S(1)}, u32[]{:S(2)}, u32[]{:S(2)}) collective-permute-start(bf16[256,2,128]{2,0,1:T(8,128)(2,1)S(1)} %copy.141), channel_id=1, source_target_pairs={{0,4},{4,8},{8,12},{1,5},{5,9},{9,13},{2,6},{6,10},{10,14},{3,7},{... | collective-permute-start | bytes 393224 | tf_op jit(solution)/shard_map/ppermute | solution.py:17
  12.6 1.2 constant_dynamic-slice_fusion.1
  13.9 3.2 %collective-permute-start.2 = (bf16[256,2,128]{0,2,1:T(8,128)(2,1)S(1)}, bf16[256,2,128]{0,2,1:T(8,128)(2,1)S(1)}, u32[]{:S(2)}, u32[]{:S(2)}) collective-permute-start(bf16[256,2,128]{0,2,1:T(8,128)(2,1)S(1)} %copy.140), channel_id=1, source_target_pairs={{0,4},{4,8},{8,12},{1,5},{5,9},{9,13},{2,6},{6,10},{10,14},{3,7},{... | collective-permute-start | bytes 393224 | tf_op jit(solution)/shard_map/ppermute | solution.py:17
  17.1 7.4 %all-gather = s32[4,1,256]{2,1,0:T(1,128)S(1)} all-gather(s32[1,1,256]{2,1,0:T(1,128)} %bitcast.191), channel_id=1, replica_groups=mesh['groups'=2,'inner'=4,'outer'=2,'heads'=2] {'inner'}, dimensions={0}, use_global_device_ids=true | all-gather | bytes 5120 | tf_op jit(solution)/shard_map/all_gather | solution.py:40
  24.6 1.0 compare_and_fusion.1
  25.5 0.9 fusion.9
  26.5 2.0 %collective-permute-start.1 = (bf16[256,2,128]{2,0,1:T(8,128)(2,1)S(1)}, bf16[256,2,128]{2,0,1:T(8,128)(2,1)S(1)}, u32[]{:S(2)}, u32[]{:S(2)}) collective-permute-start(bf16[256,2,128]{2,0,1:T(8,128)(2,1)S(1)} %collective-permute-done), channel_id=1, source_target_pairs={{0,4},{4,8},{8,12},{1,5},{5,9},{9,13},{2,6},{6,10},{10,14},{3,7},{... | collective-permute-start | bytes 393224 | tf_op jit(solution)/shard_map/ppermute | solution.py:17
  28.6 0.9 fusion.10
  29.5 1.9 %collective-permute-start.3 = (bf16[256,2,128]{0,2,1:T(8,128)(2,1)S(1)}, bf16[256,2,128]{0,2,1:T(8,128)(2,1)S(1)}, u32[]{:S(2)}, u32[]{:S(2)}) collective-permute-start(bf16[256,2,128]{0,2,1:T(8,128)(2,1)S(1)} %collective-permute-done.2), channel_id=1, source_target_pairs={{0,4},{4,8},{8,12},{1,5},{5,9},{9,13},{2,6},{6,10},{10,14},{3,7},{... | collective-permute-start | bytes 393224 | tf_op jit(solution)/shard_map/ppermute | solution.py:17
  31.5 0.9 fusion.11
  32.5 2.8 %exponential_reduce_fusion.1 = (f32[2,8,256]{2,1,0:T(8,128)S(1)}, f32[2,8,256]{2,1,0:T(8,128)S(1)}, f32[2,8,256]{2,1,0:T(8,128)S(1)}) fusion(f32[2,256,256,8]{2,1,3,0:T(8,128)S(1)} %get-tuple-element.32, f32[2,8,256]{2,1,0:T(8,128)S(1)} %maximum_maximum_fusion, pred[256,256]{0,1:T(8,128)(4,1)S(1)} %get-tuple-element.24, ...), kind=kLoop, calls=%fused_computation.16 | loop fusion | flops 12570624 | bytes 12845056 | tf_op jit(solution)/shard_map/reduce_sum | solution.py:76
  35.3 1.2 fusion.43
  36.5 2.1 %convolution_bitcast_fusion.2 = f32[256,2,128]{2,0,1:T(8,128)} fusion(bf16[256,2,8,128]{3,2,1,0:T(8,128)(2,1)S(1)} %bitcast.182, f32[2,256,256,8]{2,1,3,0:T(8,128)S(1)} %get-tuple-element.30, f32[2,8,256]{2,1,0:T(8,128)S(1)} %log_add_fusion, pred[256,256]{0,1:T(8,128)(4,1)S(1)} %get-tuple-element.26), kind=kOutput, calls=%fused_computation.29 | convolution fusion | flops 272629760 | bytes 5586944 | tf_op jit(solution)/shard_map/gjtw,tgjd->wgd/dot_general | solution.py:112
  38.6 1.2 collective-permute-start.7
  39.8 1.2 fusion.32
  41.0 1.3 add_convert_fusion.1
  42.3 1.1 copy.102
  43.4 2.2 %multiply_reduce_fusion = f32[256,16]{1,0:T(8,128)S(1)} fusion(bf16[256,16,128]{2,1,0:T(8,128)(2,1)S(1)} %copy.102, bf16[256,16,128]{2,1,0:T(8,128)(2,1)} %param.8), kind=kLoop, calls=%fused_computation.25 | loop fusion | flops 2093056 | bytes 2113536 | tf_op jit(solution)/shard_map/reduce_sum | solution.py:86
  45.7 4.3 %fusion.5 = bf16[2,8,256,256]{2,3,1,0:T(8,128)(2,1)S(1)} fusion(f32[2,256,256,8]{2,1,3,0:T(8,128)} %copy-done.3, f32[2,8,256]{2,1,0:T(8,128)S(1)} %bitcast.187, f32[2,8,256]{2,1,0:T(8,128)S(1)} %log_add_fusion, pred[256,256]{0,1:T(8,128)(4,1)S(1)} %get-tuple-element.26, bf16[256,2,8,128]{3,2,1,0:T(8,128)(2,1)} %bitcast.181, bf16[256,2,128]{0,2,1:T(8,128)(2,1)} %copy-done.16), kind=kOutput, calls=%fused_computation.8 | convolution fusion | flops 275775488 | bytes 7569408 | tf_op jit(solution)/shard_map/tgjd,wgd->gjtw/dot_general | solution.py:100
  50.0 0.7 convolution_bitcast_fusion.5
  50.9 1.7 %fusion.3 = bf16[2,8,256,256]{2,3,1,0:T(8,128)(2,1)S(1)} fusion(f32[2,256,256,8]{2,1,3,0:T(8,128)S(1)} %copy-done.2, f32[2,8,256]{2,1,0:T(8,128)S(1)} %bitcast.188, f32[2,8,256]{2,1,0:T(8,128)S(1)} %log_add_fusion, pred[256,256]{0,1:T(8,128)(4,1)S(1)} %get-tuple-element.24, bf16[256,2,8,128]{3,2,1,0:T(8,128)(2,1)S(1)} %bitcast.183, ...), kind=kOutput, calls=%fused_computation.5 | convolution fusion | flops 275775488 | bytes 7569408 | tf_op jit(solution)/shard_map/tgjd,wgd->gjtw/dot_general | solution.py:100
  52.6 0.4 copy-done.5
  53.0 1.7 %fusion.1 = bf16[2,8,256,256]{2,3,1,0:T(8,128)(2,1)S(1)} fusion(f32[2,256,256,8]{2,1,3,0:T(8,128)S(1)} %copy-done.5, f32[2,8,256]{2,1,0:T(8,128)S(1)} %bitcast.189, f32[2,8,256]{2,1,0:T(8,128)S(1)} %log_add_fusion, pred[256,256]{0,1:T(8,128)(4,1)S(1)} %get-tuple-element.25, bf16[256,2,8,128]{3,2,1,0:T(8,128)(2,1)S(1)} %bitcast.184, ...), kind=kOutput, calls=%fused_computation.2 | convolution fusion | flops 275775488 | bytes 7569408 | tf_op jit(solution)/shard_map/tgjd,wgd->gjtw/dot_general | solution.py:100
  54.6 1.4 convolution_bitcast_fusion
  56.1 2.3 %fusion.13 = f32[256,2,128]{2,0,1:T(8,128)S(1)} fusion(f32[256,2,128]{2,0,1:T(8,128)} %collective-permute-done.7, bf16[256,2,8,128]{3,2,1,0:T(8,128)(2,1)S(1)} %bitcast.186, f32[2,256,256,8]{2,1,3,0:T(8,128)S(1)} %copy-done.2, f32[2,8,256]{2,1,0:T(8,128)S(1)} %log_add_fusion, pred[256,256]{0,1:T(8,128)(4,1)S(1)} %get-tuple-element.24), kind=kOutput, calls=%fused_computation.34 | convolution fusion | flops 272695296 | bytes 5849088 | tf_op jit(solution)/shard_map/gjtw,tgjd->wgd/dot_general | solution.py:112
  58.4 0.8 collective-permute-start.8
  59.2 0.7 fusion.12
  59.9 1.8 %collective-permute-start.5 = (f32[256,2,128]{2,0,1:T(8,128)S(1)}, f32[256,2,128]{2,0,1:T(8,128)S(1)}, u32[]{:S(2)}, u32[]{:S(2)}) collective-permute-start(f32[256,2,128]{2,0,1:T(8,128)S(1)} %fusion.12), channel_id=1, source_target_pairs={{12,0},{0,4},{4,8},{8,12},{13,1},{1,5},{5,9},{9,13},{14,2},{2,6},{... | collective-permute-start | bytes 786440 | tf_op jit(solution)/shard_map/ppermute | solution.py:23
  61.8 0.7 convolution_bitcast_fusion.3
  62.5 3.6 %collective-permute-done.8 = f32[256,2,128]{2,0,1:T(8,128)S(1)} collective-permute-done((f32[256,2,128]{2,0,1:T(8,128)S(1)}, f32[256,2,128]{2,0,1:T(8,128)S(1)}, u32[]{:S(2)}, u32[]{:S(2)}) %collective-permute-start.8) | collective-permute-done | bytes 262176 | tf_op jit(solution)/shard_map/ppermute | solution.py:23
  66.2 3.5 %collective-permute-done.5 = f32[256,2,128]{2,0,1:T(8,128)S(1)} collective-permute-done((f32[256,2,128]{2,0,1:T(8,128)S(1)}, f32[256,2,128]{2,0,1:T(8,128)S(1)}, u32[]{:S(2)}, u32[]{:S(2)}) %collective-permute-start.5) | collective-permute-done | bytes 262176 | tf_op jit(solution)/shard_map/ppermute | solution.py:23
  69.7 0.7 add_convert_fusion.3
  70.4 0.2 collective-permute-start.6
  70.6 0.5 fusion.39
  71.1 10.6 %collective-permute-done.9 = bf16[256,2,128]{2,0,1:T(8,128)(2,1)S(1)} collective-permute-done((bf16[256,2,128]{2,0,1:T(8,128)(2,1)S(1)}, bf16[256,2,128]{2,0,1:T(8,128)(2,1)S(1)}, u32[]{:S(2)}, u32[]{:S(2)}) %collective-permute-start.9) | collective-permute-done | bytes 131104 | tf_op jit(solution)/shard_map/ppermute | solution.py:23
  81.7 0.1 copy.101
  81.9 0.9 broadcast_in_dim.30.clone.1
  82.8 7.0 %dynamic_update_slice.7 = bf16[256,8,128]{2,1,0:T(8,128)(2,1)} dynamic-update-slice(bf16[256,8,128]{2,1,0:T(8,128)(2,1)} %broadcast_in_dim.30.clone.1, bf16[256,2,128]{2,1,0:T(2,128)(2,1)S(1)} %copy.101, s32[]{:T(128)} %constant.15.clone.1, s32[]{:T(128)S(6)} %select_n.31, s32[]{:T(128)} %constant.15.clone.1) | dynamic-update-slice | bytes 262148 | tf_op jit(solution)/shard_map/dynamic_update_slice | solution.py:124
  89.8 1.0 copy.97
  90.9 0.9 broadcast_in_dim.30.clone
  91.7 7.0 %dynamic_update_slice.6 = bf16[256,8,128]{2,1,0:T(8,128)(2,1)} dynamic-update-slice(bf16[256,8,128]{2,1,0:T(8,128)(2,1)} %broadcast_in_dim.30.clone, bf16[256,2,128]{2,1,0:T(2,128)(2,1)S(1)} %copy.97, s32[]{:T(128)} %constant.15.clone.1, s32[]{:T(128)S(6)} %select_n.31, s32[]{:T(128)} %constant.15.clone.1) | dynamic-update-slice | bytes 262148 | tf_op jit(solution)/shard_map/dynamic_update_slice | solution.py:123
  98.8 2.2 %fusion.36 = f32[2,128,8,256]{3,1,2,0:T(8,128)S(1)} fusion(bf16[2,8,256,256]{2,3,1,0:T(8,128)(2,1)} %copy-done.6, bf16[256,2,128]{2,0,1:T(8,128)(2,1)S(1)} %copy-done.15), kind=kOutput, calls=%fused_computation.62 | convolution fusion | flops 268435456 | bytes 4325376 | tf_op jit(solution)/shard_map/gjtw,wgd->tgjd/dot_general | solution.py:106
  101.1 1.7 %add_convert_fusion = bf16[2,128,8,256]{3,1,2,0:T(8,128)(2,1)} fusion(f32[2,128,8,256]{3,1,2,0:T(8,128)S(1)} %fusion.39, f32[2,128,8,256]{3,1,2,0:T(8,128)S(1)} %fusion.36, bf16[2,8,256,256]{2,3,1,0:T(8,128)(2,1)S(1)} %copy-done.9, bf16[256,2,128]{2,0,1:T(8,128)(2,1)S(1)} %copy-done.13), kind=kOutput, calls=%fused_computation.24 | convolution fusion | flops 270008320 | bytes 7471104 | tf_op jit(solution)/shard_map/gjtw,wgd->tgjd/dot_general | solution.py:106
  102.7 2.6 %copy.103 = bf16[256,16,128]{2,1,0:T(8,128)(2,1)} copy(bf16[256,16,128]{0,2,1:T(8,128)(2,1)} %bitcast.179) | data formatting | bytes 2097152
  105.4 29.5 %all-reduce.3.cloned.1.call-done = (bf16[256,8,128]{2,1,0:T(8,128)(2,1)}, bf16[256,8,128]{2,1,0:T(8,128)(2,1)}) async-done(((bf16[256,8,128]{2,1,0:T(8,128)(2,1)}, bf16[256,8,128]{2,1,0:T(8,128)(2,1)}), (bf16[256,8,128]{2,1,0:T(8,128)(2,1)}, bf16[256,8,128]{2,1,0:T(8,128)(2,1)})) %all-reduce.3.cloned.1.call-update) | async-done | bytes 1048592 | tf_op jit(solution)/shard_map/psum | solution.py:126
  134.8 1.9 %copy.186 = bf16[256,8,128]{2,1,0:T(8,128)(2,1)} copy(bf16[256,8,128]{2,1,0:T(8,128)(2,1)} %get-tuple-element.38) | data formatting | bytes 1048576
  136.7 1.9 %copy.187 = bf16[256,8,128]{2,1,0:T(8,128)(2,1)} copy(bf16[256,8,128]{2,1,0:T(8,128)(2,1)} %get-tuple-element.39) | data formatting | bytes 1048576
  (60 shorter events, 0.6 us)
Async XLA Ops:
  7.2 18.4 %copy-start = (bf16[256,16,128]{2,1,0:T(8,128)(2,1)S(1)}, bf16[256,16,128]{2,1,0:T(8,128)(2,1)}, u32[]{:S(2)}) copy-start(bf16[256,16,128]{2,1,0:T(8,128)(2,1)} %param.5) | copy-start | bytes 3145732
  7.2 127.6 %all-reduce.3.cloned.1.call-start = ((), (), s32[]{:S(2)}) async-start(), calls=%async_computation | async-start | bytes 2097152 | tf_op jit(solution)/shard_map/psum | solution.py:126
  8.5 18.0 %collective-permute-start = (bf16[256,2,128]{2,0,1:T(8,128)(2,1)S(1)}, bf16[256,2,128]{2,0,1:T(8,128)(2,1)S(1)}, u32[]{:S(2)}, u32[]{:S(2)}) collective-permute-start(bf16[256,2,128]{2,0,1:T(8,128)(2,1)S(1)} %copy.141), channel_id=1, source_target_pairs={{0,4},{4,8},{8,12},{1,5},{5,9},{9,13},{2,6},{6,10},{10,14},{3,7},{... | collective-permute-start | bytes 393224 | tf_op jit(solution)/shard_map/ppermute | solution.py:17
  13.9 21.4 %copy-start.16 = (bf16[256,2,128]{0,2,1:T(8,128)(2,1)}, bf16[256,2,128]{0,2,1:T(8,128)(2,1)S(1)}, u32[]{:S(2)}) copy-start(bf16[256,2,128]{0,2,1:T(8,128)(2,1)S(1)} %copy.140) | copy-start | bytes 393220
  13.9 15.6 %collective-permute-start.2 = (bf16[256,2,128]{0,2,1:T(8,128)(2,1)S(1)}, bf16[256,2,128]{0,2,1:T(8,128)(2,1)S(1)}, u32[]{:S(2)}, u32[]{:S(2)}) collective-permute-start(bf16[256,2,128]{0,2,1:T(8,128)(2,1)S(1)} %copy.140), channel_id=1, source_target_pairs={{0,4},{4,8},{8,12},{1,5},{5,9},{9,13},{2,6},{6,10},{10,14},{3,7},{... | collective-permute-start | bytes 393224 | tf_op jit(solution)/shard_map/ppermute | solution.py:17
  26.5 10.0 %copy-start.3 = (f32[2,256,256,8]{2,1,3,0:T(8,128)}, f32[2,256,256,8]{2,1,3,0:T(8,128)S(1)}, u32[]{:S(2)}) copy-start(f32[2,256,256,8]{2,1,3,0:T(8,128)S(1)} %get-tuple-element.30) | copy-start | bytes 12582916
  26.5 5.9 %copy-start.14 = (bf16[256,2,128]{2,0,1:T(8,128)(2,1)}, bf16[256,2,128]{2,0,1:T(8,128)(2,1)S(1)}, u32[]{:S(2)}) copy-start(bf16[256,2,128]{2,0,1:T(8,128)(2,1)S(1)} %collective-permute-done) | copy-start | bytes 393220
  26.5 4.9 %collective-permute-start.1 = (bf16[256,2,128]{2,0,1:T(8,128)(2,1)S(1)}, bf16[256,2,128]{2,0,1:T(8,128)(2,1)S(1)}, u32[]{:S(2)}, u32[]{:S(2)}) collective-permute-start(bf16[256,2,128]{2,0,1:T(8,128)(2,1)S(1)} %collective-permute-done), channel_id=1, source_target_pairs={{0,4},{4,8},{8,12},{1,5},{5,9},{9,13},{2,6},{6,10},{10,14},{3,7},{... | collective-permute-start | bytes 393224 | tf_op jit(solution)/shard_map/ppermute | solution.py:17
  29.5 10.3 %copy-start.1 = (f32[2,256,256,8]{2,1,3,0:T(8,128)}, f32[2,256,256,8]{2,1,3,0:T(8,128)S(1)}, u32[]{:S(2)}) copy-start(f32[2,256,256,8]{2,1,3,0:T(8,128)S(1)} %get-tuple-element.32) | copy-start | bytes 12582916
  29.5 10.2 %copy-start.19 = (bf16[256,2,128]{0,2,1:T(8,128)(2,1)}, bf16[256,2,128]{0,2,1:T(8,128)(2,1)S(1)}, u32[]{:S(2)}) copy-start(bf16[256,2,128]{0,2,1:T(8,128)(2,1)S(1)} %collective-permute-done.2) | copy-start | bytes 393220
  29.5 11.4 %collective-permute-start.3 = (bf16[256,2,128]{0,2,1:T(8,128)(2,1)S(1)}, bf16[256,2,128]{0,2,1:T(8,128)(2,1)S(1)}, u32[]{:S(2)}, u32[]{:S(2)}) collective-permute-start(bf16[256,2,128]{0,2,1:T(8,128)(2,1)S(1)} %collective-permute-done.2), channel_id=1, source_target_pairs={{0,4},{4,8},{8,12},{1,5},{5,9},{9,13},{2,6},{6,10},{10,14},{3,7},{... | collective-permute-start | bytes 393224 | tf_op jit(solution)/shard_map/ppermute | solution.py:17
  31.5 3.8 %copy-start.12 = (bf16[256,2,128]{2,0,1:T(8,128)(2,1)}, bf16[256,2,128]{2,0,1:T(8,128)(2,1)S(1)}, u32[]{:S(2)}) copy-start(bf16[256,2,128]{2,0,1:T(8,128)(2,1)S(1)} %collective-permute-done.1) | copy-start | bytes 393220
  32.4 8.6 %copy-start.4 = (f32[2,256,256,8]{2,1,3,0:T(8,128)}, f32[2,256,256,8]{2,1,3,0:T(8,128)S(1)}, u32[]{:S(2)}) copy-start(f32[2,256,256,8]{2,1,3,0:T(8,128)S(1)} %get-tuple-element.28) | copy-start | bytes 12582916
  35.3 1.3 copy-start.10
  38.6 17.4 %collective-permute-start.7 = (f32[256,2,128]{2,0,1:T(8,128)}, f32[256,2,128]{2,0,1:T(8,128)}, u32[]{:S(2)}, u32[]{:S(2)}) collective-permute-start(f32[256,2,128]{2,0,1:T(8,128)} %convolution_bitcast_fusion.2), channel_id=1, source_target_pairs={{12,0},{0,4},{4,8},{8,12},{13,1},{1,5},{5,9},{9,13},{14,2},{2,6},{... | collective-permute-start | bytes 786440 | tf_op jit(solution)/shard_map/ppermute | solution.py:23
  41.0 1.3 copy-start.17
  43.4 6.6 %copy-start.7 = (bf16[256,16,128]{2,1,0:T(8,128)(2,1)}, bf16[256,16,128]{2,1,0:T(8,128)(2,1)S(1)}, u32[]{:S(2)}) copy-start(bf16[256,16,128]{2,1,0:T(8,128)(2,1)S(1)} %copy.102) | copy-start | bytes 3145732
  45.7 5.2 %copy-start.2 = (f32[2,256,256,8]{2,1,3,0:T(8,128)S(1)}, f32[2,256,256,8]{2,1,3,0:T(8,128)}, u32[]{:S(2)}) copy-start(f32[2,256,256,8]{2,1,3,0:T(8,128)} %copy-done.1) | copy-start | bytes 12582916
  45.7 5.2 %copy-start.11 = (bf16[256,16,128]{2,1,0:T(8,128)(2,1)S(1)}, bf16[256,16,128]{2,1,0:T(8,128)(2,1)}, u32[]{:S(2)}) copy-start(bf16[256,16,128]{2,1,0:T(8,128)(2,1)} %param.8) | copy-start | bytes 3145732
  45.7 5.2 %copy-start.20 = (bf16[256,2,128]{0,2,1:T(8,128)(2,1)S(1)}, bf16[256,2,128]{0,2,1:T(8,128)(2,1)}, u32[]{:S(2)}) copy-start(bf16[256,2,128]{0,2,1:T(8,128)(2,1)} %copy-done.19) | copy-start | bytes 393220
  50.8 2.2 %copy-start.5 = (f32[2,256,256,8]{2,1,3,0:T(8,128)S(1)}, f32[2,256,256,8]{2,1,3,0:T(8,128)}, u32[]{:S(2)}) copy-start(f32[2,256,256,8]{2,1,3,0:T(8,128)} %copy-done.4) | copy-start | bytes 12582916
  50.8 2.2 %copy-start.18 = (bf16[256,2,128]{0,2,1:T(8,128)(2,1)S(1)}, bf16[256,2,128]{0,2,1:T(8,128)(2,1)}, u32[]{:S(2)}) copy-start(bf16[256,2,128]{0,2,1:T(8,128)(2,1)} %copy-done.17) | copy-start | bytes 393220
  50.8 8.4 %collective-permute-start.4 = (f32[256,2,128]{2,0,1:T(8,128)S(1)}, f32[256,2,128]{2,0,1:T(8,128)S(1)}, u32[]{:S(2)}, u32[]{:S(2)}) collective-permute-start(f32[256,2,128]{2,0,1:T(8,128)S(1)} %convolution_bitcast_fusion.5), channel_id=1, source_target_pairs={{12,0},{0,4},{4,8},{8,12},{13,1},{1,5},{5,9},{9,13},{14,2},{2,6},{... | collective-permute-start | bytes 786440 | tf_op jit(solution)/shard_map/ppermute | solution.py:23
  52.9 6.3 %copy-start.6 = (bf16[2,8,256,256]{2,3,1,0:T(8,128)(2,1)}, bf16[2,8,256,256]{2,3,1,0:T(8,128)(2,1)S(1)}, u32[]{:S(2)}) copy-start(bf16[2,8,256,256]{2,3,1,0:T(8,128)(2,1)S(1)} %fusion.3) | copy-start | bytes 6291460
  54.6 7.1 %copy-start.8 = (bf16[2,8,256,256]{2,3,1,0:T(8,128)(2,1)}, bf16[2,8,256,256]{2,3,1,0:T(8,128)(2,1)S(1)}, u32[]{:S(2)}) copy-start(bf16[2,8,256,256]{2,3,1,0:T(8,128)(2,1)S(1)} %fusion.1) | copy-start | bytes 6291460
  58.4 7.7 %collective-permute-start.8 = (f32[256,2,128]{2,0,1:T(8,128)S(1)}, f32[256,2,128]{2,0,1:T(8,128)S(1)}, u32[]{:S(2)}, u32[]{:S(2)}) collective-permute-start(f32[256,2,128]{2,0,1:T(8,128)S(1)} %fusion.13), channel_id=1, source_target_pairs={{12,0},{0,4},{4,8},{8,12},{13,1},{1,5},{5,9},{9,13},{14,2},{2,6},{... | collective-permute-start | bytes 786440 | tf_op jit(solution)/shard_map/ppermute | solution.py:23
  59.9 9.8 %collective-permute-start.5 = (f32[256,2,128]{2,0,1:T(8,128)S(1)}, f32[256,2,128]{2,0,1:T(8,128)S(1)}, u32[]{:S(2)}, u32[]{:S(2)}) collective-permute-start(f32[256,2,128]{2,0,1:T(8,128)S(1)} %fusion.12), channel_id=1, source_target_pairs={{12,0},{0,4},{4,8},{8,12},{13,1},{1,5},{5,9},{9,13},{14,2},{2,6},{... | collective-permute-start | bytes 786440 | tf_op jit(solution)/shard_map/ppermute | solution.py:23
  66.1 32.7 %copy-start.15 = (bf16[256,2,128]{2,0,1:T(8,128)(2,1)S(1)}, bf16[256,2,128]{2,0,1:T(8,128)(2,1)}, u32[]{:S(2)}) copy-start(bf16[256,2,128]{2,0,1:T(8,128)(2,1)} %copy-done.14) | copy-start | bytes 393220
  66.2 15.6 %collective-permute-start.9 = (bf16[256,2,128]{2,0,1:T(8,128)(2,1)S(1)}, bf16[256,2,128]{2,0,1:T(8,128)(2,1)S(1)}, u32[]{:S(2)}, u32[]{:S(2)}) collective-permute-start(bf16[256,2,128]{2,0,1:T(8,128)(2,1)S(1)} %add_convert_fusion.2), channel_id=1, source_target_pairs={{8,0},{12,4},{0,8},{4,12},{9,1},{13,5},{1,9},{5,13},{10,2},{14,6},... | collective-permute-start | bytes 393224 | tf_op jit(solution)/shard_map/ppermute | solution.py:23
  70.4 19.4 %collective-permute-start.6 = (bf16[256,2,128]{2,0,1:T(8,128)(2,1)}, bf16[256,2,128]{2,0,1:T(8,128)(2,1)}, u32[]{:S(2)}, u32[]{:S(2)}) collective-permute-start(bf16[256,2,128]{2,0,1:T(8,128)(2,1)} %add_convert_fusion.3), channel_id=1, source_target_pairs={{8,0},{12,4},{0,8},{4,12},{9,1},{13,5},{1,9},{5,13},{10,2},{14,6},... | collective-permute-start | bytes 393224 | tf_op jit(solution)/shard_map/ppermute | solution.py:23
  71.1 30.0 %copy-start.13 = (bf16[256,2,128]{2,0,1:T(8,128)(2,1)S(1)}, bf16[256,2,128]{2,0,1:T(8,128)(2,1)}, u32[]{:S(2)}) copy-start(bf16[256,2,128]{2,0,1:T(8,128)(2,1)} %copy-done.12) | copy-start | bytes 393220
  98.8 2.2 %copy-start.9 = (bf16[2,8,256,256]{2,3,1,0:T(8,128)(2,1)S(1)}, bf16[2,8,256,256]{2,3,1,0:T(8,128)(2,1)}, u32[]{:S(2)}) copy-start(bf16[2,8,256,256]{2,3,1,0:T(8,128)(2,1)} %copy-done.8) | copy-start | bytes 6291460
Sparse Core Ops, SparseCore 0:
  98.9 35.8 all-reduce.2
where the time goes:
time: 147 us; the launch traced here: 145 us
  waiting for transfers between devices  47.2 us (32%)
  local copies, waits for them, and re-layouts  27.6 us (19%)
  matrix products  26.5 us (18%)
  starting transfers between devices  15.4 us (10%)
  between operations  14.6 us (10%)
  blocking collectives  7.36 us (5%)
  other arithmetic  6.79 us (5%)
    psum x1, waiting for transfers between devices, shards(): lax.psum(key_placed.astype(jnp.bfloat16), ('outer', 'heads'))  29.5 us
    ppermute x6, waiting for transfers between devices, passed_along_2(): return lax.ppermute(block, axis, route)  17.7 us
    ppermute x4, starting transfers between devices, passed_along(): return lax.ppermute(array, axis, pairs)  11.2 us
    unnamed x48, local copies, waits for them, and re-layouts  8.06 us
    dot_general x3, matrix products, shards(): jnp.einsum('tgjd,wgd->gjtw', grad_grouped, value_block, preferred_element...  7.66 us
    all_gather x1, blocking collectives, shards(): segs_all = lax.all_gather(seg_ids, 'inner', axis=0, tiled=True)  7.36 us
    dynamic_update_slice x1, local copies, waits for them, and re-layouts, shards(): lax.dynamic_update_slice_in_dim(empty_full, grad_acc[1], kv_slot, 1)  7.05 us
    dynamic_update_slice x1, local copies, waits for them, and re-layouts, shards(): lax.dynamic_update_slice_in_dim(empty_full, grad_acc[0], kv_slot, 1)  7.05 us
  transfers between devices with their start and end apart: 11, of which 4 were waited for; matrix products, arithmetic and copies ran while one was open for 32% of the time, Pallas kernels for 0%

commit v1 on v0

v1 whole, which is shorter than its diff:
```python
import functools
import math

import jax
import jax.numpy as jnp
from jax import lax
from jax.experimental import pallas as pl
from jax.experimental.pallas import tpu as pltpu
from jax.sharding import PartitionSpec as P

GROUP = 8
MASKED = -1e30
MESH = pl.DeviceIdType.MESH


def dot(a, b, ca, cb):
    return lax.dot_general(
        a, b, (((ca,), (cb,)), ((), ())), preferred_element_type=jnp.float32
    )


def kernel(
    cfg, q_ref, do_ref, kv_ref, segrow_ref, segq_ref,
    out_ref, dq_ref, grads_ref,
    kv_buf, seg_buf, kcat, vcat, segcat, p_buf, ds_buf, dkcat, dvcat,
    back_send, back_recv, gather, share_recv,
    kv_ssem, kv_rsem, seg_ssem, seg_rsem, b_ssem, b_rsem, g_ssem, g_rsem, h_ssem, h_rsem,
):
    n_in, reach, n_out, kvl, gh, share, tok = cfg
    head_dim = q_ref.shape[-1]
    half = tok // 2
    scale = head_dim ** (-0.5)
    width = half + half + tok * (reach - 1)
    pos = lax.axis_index("inner")
    outer = lax.axis_index("outer")
    core = lax.axis_index("heads")

    barrier = pltpu.get_barrier_semaphore()

    @pl.when(pos > 0)
    def _():
        pl.semaphore_signal(barrier, inc=1, device_id={"inner": pos - 1}, device_id_type=MESH)

    @pl.when(pos < n_in - 1)
    def _():
        pl.semaphore_signal(barrier, inc=1, device_id={"inner": pos + 1}, device_id_type=MESH)

    pl.semaphore_signal(barrier, inc=1, device_id={"heads": 1 - core}, device_id_type=MESH)
    for o in range(1, n_out):
        pl.semaphore_signal(
            barrier, inc=1, device_id={"outer": lax.rem(outer + o, n_out)}, device_id_type=MESH
        )
    ends = jnp.where(pos > 0, 1, 0) + jnp.where(pos < n_in - 1, 1, 0)
    pl.semaphore_wait(barrier, ends + n_out)

    def kv_copy(g, d):
        src = kv_ref.at[g] if d == 1 else kv_buf.at[g, d - 2]
        return pltpu.make_async_remote_copy(
            src_ref=src, dst_ref=kv_buf.at[g, d - 1],
            send_sem=kv_ssem.at[g, d - 1], recv_sem=kv_rsem.at[g, d - 1],
            device_id={"inner": pos + 1}, device_id_type=MESH,
        )

    def seg_copy(d):
        src = segrow_ref if d == 1 else seg_buf.at[d - 2]
        return pltpu.make_async_remote_copy(
            src_ref=src, dst_ref=seg_buf.at[d - 1],
            send_sem=seg_ssem.at[d - 1], recv_sem=seg_rsem.at[d - 1],
            device_id={"inner": pos + 1}, device_id_type=MESH,
        )

    def sends(d):
        return (pos + 1 < n_in) & (pos >= d - 1)

    def back_receives(d):
        return (pos + 1 < n_in) & (pos + 1 >= d)

    def start_hop(d):
        @pl.when(sends(d))
        def _():
            seg_copy(d).start()
            for g in range(kvl):
                kv_copy(g, d).start()

    for d in range(1, reach + 1):
        @pl.when(pos < d)
        def _():
            seg_buf[d - 1] = jnp.full(seg_buf.shape[1:], -1, jnp.int32)
            for g in range(kvl):
                kv_buf[g, d - 1] = jnp.zeros(kv_buf.shape[2:], kv_buf.dtype)

        @pl.when(jnp.logical_not(back_receives(d)))
        def _():
            for g in range(kvl):
                back_recv[g, d - 1] = jnp.zeros(back_recv.shape[2:], back_recv.dtype)

    start_hop(1)
    for d in range(1, reach + 1):
        @pl.when(pos >= d)
        def _():
            seg_copy(d).wait_recv()
            kv_copy(0, d).wait_recv()
        if d < reach:
            @pl.when(sends(d + 1))
            def _():
                seg_copy(d + 1).start()
                kv_copy(0, d + 1).start()
            for g in range(1, kvl):
                @pl.when(pos >= d)
                def _():
                    kv_copy(g, d).wait_recv()

                @pl.when(sends(d + 1))
                def _():
                    kv_copy(g, d + 1).start()

    def block(g, c, d, rows):
        if d == 0:
            return kv_ref[g, c, rows, :]
        return kv_buf[g, d - 1, c, rows, :]

    low, high = slice(0, half), slice(half, tok)
    mixes = (low, high)

    for hf in range(2):
        rest = high if hf == 0 else low
        far = reach if hf == 0 else 0
        seg0 = segrow_ref[:, mixes[hf]]
        segr = seg_buf[reach - 1, :, mixes[hf]]
        segcat[hf, :, 0:half] = seg0
        segcat[hf, :, half:tok] = segr
        segcat[hf, :, tok:tok + half] = segrow_ref[:, rest] if far == 0 else seg_buf[reach - 1, :, rest]
        for d in range(1, reach):
            at = tok + half + (d - 1) * tok
            segcat[hf, :, at:at + tok] = seg_buf[d - 1]

    rows_half = half * gh
    rows = min(512, rows_half)
    chunks = rows_half // rows
    tokens = rows // gh

    def compute(g, hf):
        rest = high if hf == 0 else low
        far = reach if hf == 0 else 0
        for c, cat in ((0, kcat), (1, vcat)):
            cat[0:half, :] = block(g, c, 0, mixes[hf])
            cat[half:tok, :] = block(g, c, reach, mixes[hf])
            cat[tok:tok + half, :] = block(g, c, far, rest)
            for d in range(1, reach):
                at = tok + half + (d - 1) * tok
                cat[at:at + tok, :] = block(g, c, d, slice(None))

        def chunk(i, carry):
            local = pl.ds(pl.multiple_of(i * rows, rows), rows)
            where = pl.ds(pl.multiple_of(hf * rows_half + i * rows, rows), rows)
            q = q_ref[g, where, :]
            do = do_ref[g, where, :]
            row_tok = lax.broadcasted_iota(jnp.int32, (rows, half), 0) // gh + i * tokens
            causal = lax.broadcasted_iota(jnp.int32, (rows, half), 1) <= row_tok
            seg_q = segq_ref[where, :]

            def merge(full):
                return [jnp.where(causal, full[:, 0:half], full[:, half:tok])] + [
                    full[:, at:at + half] for at in range(tok, width + half, half)
                ]

            segs = [segcat[hf, 0:1, at:at + half] for at in range(0, width + half, half)]
            seg_k = [jnp.where(causal, segs[0], segs[1])] + segs[2:]
            scores = merge(dot(q, kcat[...], 1, 1))
            scores = [jnp.where(k == seg_q, s, MASKED) for k, s in zip(seg_k, scores)]
            top = jnp.max(functools.reduce(jnp.maximum, scores), 1, keepdims=True)
            es = [jnp.exp2((s - top) * (scale * math.log2(math.e))) for s in scores]
            total = jnp.sum(functools.reduce(jnp.add, es), 1, keepdims=True)
            inv = 1.0 / total
            ps = [e * inv for e in es]

            def spread(parts):
                own = jnp.where(causal, parts[0], 0.0)
                other = jnp.where(causal, 0.0, parts[0])
                return jnp.concatenate(
                    [x.astype(jnp.bfloat16) for x in [own, other] + parts[1:]], 1
                )

            pb = spread(ps)
            p_buf[local, :] = pb
            ob = dot(pb, vcat[...], 1, 0).astype(jnp.bfloat16)
            out_ref[g, where, :] = ob
            delta = jnp.sum(do.astype(jnp.float32) * ob.astype(jnp.float32), 1, keepdims=True)
            dps = merge(dot(do, vcat[...], 1, 1))
            dsb = spread([(p * scale) * (dp - delta) for p, dp in zip(ps, dps)])
            ds_buf[local, :] = dsb
            dq_ref[g, where, :] = dot(dsb, kcat[...], 1, 0).astype(jnp.bfloat16)
            return carry

        lax.fori_loop(0, chunks, chunk, 0)
        where = pl.ds(hf * rows_half, rows_half)
        dkcat[g, hf] = dot(ds_buf[...], q_ref[g, where, :], 0, 0)
        dvcat[g, hf] = dot(p_buf[...], do_ref[g, where, :], 0, 0)

    def partial(g, c, d, part):
        cat = (dkcat if c == 0 else dvcat).at[g]
        if d == 0:
            if part == 0:
                return cat[0, 0:half, :] + cat[1, tok:tok + half, :]
            return cat[1, 0:half, :]
        if d == reach:
            if part == 0:
                return cat[0, half:tok, :]
            return cat[1, half:tok, :] + cat[0, tok:tok + half, :]
        at = tok + half + (d - 1) * tok + part * half
        return cat[0, at:at + half, :] + cat[1, at:at + half, :]

    def back_copy(g, d):
        return pltpu.make_async_remote_copy(
            src_ref=back_send.at[g, d - 1], dst_ref=back_recv.at[g, d - 1],
            send_sem=b_ssem.at[g, d - 1], recv_sem=b_rsem.at[g, d - 1],
            device_id={"inner": pos - 1}, device_id_type=MESH,
        )

    def summed(ref, g, d):
        for c in range(2):
            for part in range(2):
                term = partial(g, c, d, part)
                if d < reach:
                    term = term + back_recv[g, d, c, mixes[part], :].astype(jnp.float32)
                ref[c, mixes[part], :] = term.astype(ref.dtype)

    slot = (outer * 2 + core) * kvl // share

    def final(g):
        return gather.at[slot + g]

    def outer_copy(g, o):
        return pltpu.make_async_remote_copy(
            src_ref=final(g), dst_ref=final(g),
            send_sem=g_ssem.at[g, o - 1], recv_sem=g_rsem.at[g, o - 1],
            device_id={"outer": lax.rem(outer + o, n_out)}, device_id_type=MESH,
        )

    def sibling_copy(g, o):
        src_outer = lax.rem(outer - o + n_out, n_out)
        at = gather.at[(src_outer * 2 + core) * kvl // share + g]
        return pltpu.make_async_remote_copy(
            src_ref=at, dst_ref=at,
            send_sem=h_ssem.at[g, o], recv_sem=h_rsem.at[g, o],
            device_id={"heads": 1 - core}, device_id_type=MESH,
        )

    def share_copy(g):
        return pltpu.make_async_remote_copy(
            src_ref=final(g), dst_ref=share_recv.at[g],
            send_sem=h_ssem.at[g, 0], recv_sem=h_rsem.at[g, 0],
            device_id={"heads": 1 - core}, device_id_type=MESH,
        )

    def chain_step(g, d):
        if d < reach:
            @pl.when(back_receives(d + 1))
            def _():
                back_copy(g, d + 1).wait_recv()
        if d > 0:
            summed(back_send.at[g, d - 1], g, d)

            @pl.when(pos >= d)
            def _():
                back_copy(g, d).start()
            return
        summed(final(g), g, 0)
        if share > 1:
            copy = share_copy(g)
            copy.start()
            copy.wait()
            final(g)[...] = (
                final(g)[...].astype(jnp.float32) + share_recv[g].astype(jnp.float32)
            ).astype(gather.dtype)
        else:
            sibling_copy(g, 0).start()
        for o in range(1, n_out):
            outer_copy(g, o).start()

    for g in range(kvl):
        if g > 0:
            @pl.when(pos >= reach)
            def _():
                kv_copy(g, reach).wait_recv()
        for hf in range(2):
            compute(g, hf)
            if g > 0 and hf == 0:
                for d in range(reach - 1, 0, -1):
                    chain_step(g - 1, d)
        if g > 0:
            chain_step(g - 1, 0)
        chain_step(g, reach)
    for d in range(reach - 1, -1, -1):
        chain_step(kvl - 1, d)

    for g in range(kvl):
        for o in range(1, n_out):
            outer_copy(g, o).wait_recv()
            if share == 1:
                sibling_copy(g, o).start()
    if share == 1:
        for g in range(kvl):
            for o in range(n_out):
                sibling_copy(g, o).wait_recv()
    grads_ref[...] = gather[...]

    for d in range(1, reach + 1):
        @pl.when(sends(d))
        def _():
            seg_copy(d).wait_send()
            for g in range(kvl):
                kv_copy(g, d).wait_send()

        @pl.when(pos >= d)
        def _():
            for g in range(kvl):
                back_copy(g, d).wait_send()
    for g in range(kvl):
        for o in range(1, n_out):
            outer_copy(g, o).wait_send()
        if share == 1:
            for o in range(n_out):
                sibling_copy(g, o).wait_send()


def shards(queries, keys, values, grad_out, seg_ids):
    tok, heads, depth = queries.shape
    kv_total = keys.shape[1]
    gh = min(GROUP, heads)
    kvl = heads // gh
    share = GROUP // gh
    n_in, n_out = lax.axis_size("inner"), lax.axis_size("outer")
    reach = n_in // 2
    rows = tok * gh
    width = tok + (tok // 2) + tok * (reach - 1)
    slot = lax.axis_index(("outer", "heads")) * heads // GROUP
    wire = jnp.bfloat16 if reach <= 2 else jnp.float32

    def grouped(x):
        return x.reshape(tok, kvl, gh, depth).transpose(1, 0, 2, 3).reshape(kvl, rows, depth)

    def ungrouped(x):
        return x.reshape(kvl, tok, gh, depth).transpose(1, 0, 2, 3).reshape(tok, heads, depth)

    kv_own = jnp.stack(
        [lax.dynamic_slice_in_dim(x, slot, kvl, 1).transpose(1, 0, 2) for x in (keys, values)], 1
    )
    seg_row = jnp.broadcast_to(seg_ids[None, :], (8, tok))
    seg_q = jnp.broadcast_to(jnp.repeat(seg_ids, gh)[:, None], (rows, tok // 2))
    bf, f32 = jnp.bfloat16, jnp.float32
    dma = pltpu.SemaphoreType.DMA
    vmem = pl.BlockSpec(memory_space=pltpu.VMEM)
    out, dq, grads = pl.pallas_call(
        functools.partial(kernel, (n_in, reach, n_out, kvl, gh, share, tok)),
        out_shape=(
            jax.ShapeDtypeStruct((kvl, rows, depth), bf),
            jax.ShapeDtypeStruct((kvl, rows, depth), bf),
            jax.ShapeDtypeStruct((kv_total, 2, tok, depth), bf),
        ),
        in_specs=[vmem] * 5,
        out_specs=(vmem,) * 3,
        scratch_shapes=[
            pltpu.VMEM((kvl, reach, 2, tok, depth), bf),
            pltpu.VMEM((reach, 8, tok), jnp.int32),
            pltpu.VMEM((width, depth), bf),
            pltpu.VMEM((width, depth), bf),
            pltpu.VMEM((2, 8, width), jnp.int32),
            pltpu.VMEM((rows // 2, width), bf),
            pltpu.VMEM((rows // 2, width), bf),
            pltpu.VMEM((kvl, 2, width, depth), f32),
            pltpu.VMEM((kvl, 2, width, depth), f32),
            pltpu.VMEM((kvl, reach, 2, tok, depth), wire),
            pltpu.VMEM((kvl, reach, 2, tok, depth), wire),
            pltpu.VMEM((kv_total, 2, tok, depth), bf),
            pltpu.VMEM((kvl, 2, tok, depth), bf),
            dma((kvl, reach)), dma((kvl, reach)),
            dma((reach,)), dma((reach,)),
            dma((kvl, reach)), dma((kvl, reach)),
            dma((kvl, n_out)), dma((kvl, n_out)),
            dma((kvl, n_out)), dma((kvl, n_out)),
        ],
        compiler_params=pltpu.CompilerParams(
            collective_id=0, has_side_effects=True, vmem_limit_bytes=48 * 2**20
        ),
    )(grouped(queries), grouped(grad_out), kv_own, seg_row, seg_q)
    return (
        ungrouped(out),
        ungrouped(dq),
        grads[:, 0].transpose(1, 0, 2),
        grads[:, 1].transpose(1, 0, 2),
    )


def solution(mesh):
    act = P(("groups", "inner"), ("outer", "heads"), None)
    kv = P(("groups", "inner"), None, None)
    return jax.shard_map(
        shards,
        mesh=mesh,
        in_specs=(act, kv, kv, act, P(("groups", "inner"))),
        out_specs=(act, act, kv, kv),
        check_vma=False,
    )
```

time: 147 us -> 57.6 us (0.39)
  Pallas kernels: 0 us -> 47.8 us
  waiting for transfers between devices: 47.2 us -> 0 us
  matrix products: 26.5 us -> 0 us
  local copies, waits for them, and re-layouts: 27.6 us -> 8.81 us
  starting transfers between devices: 15.4 us -> 0 us
  between operations: 14.6 us -> 0.74 us
  blocking collectives: 7.36 us -> 0 us
  other arithmetic: 6.79 us -> 0.03 us
    pallas_call x0 -> x1, Pallas kernels: none -> 47.8 us  [shards(): pl.pallas_call(functools.partial(kernel, (n_in, reach, n_out, kvl, gh, sh...]
    psum x1 -> x0, waiting for transfers between devices: 29.5 us -> none  [shards(): lax.psum(key_placed.astype(jnp.bfloat16), ('outer', 'heads'))]
    dot_general x18 -> x0, matrix products: 26.5 us -> none  [the longest x3 7.66 us: shards(): jnp.einsum('tgjd,wgd->gjtw', grad_grouped, value_block, preferred_element...]
    ppermute x10 -> x0, waiting for transfers between devices: 17.7 us -> none  [the longest x6 17.7 us: passed_along_2(): return lax.ppermute(block, axis, route)]
    ppermute x10 -> x0, starting transfers between devices: 15.3 us -> none  [the longest x4 11.2 us: passed_along(): return lax.ppermute(array, axis, pairs)]
    dynamic_update_slice x2 -> x0, local copies, waits for them, and re-layouts: 14.1 us -> none  [the longest x1 7.05 us: shards(): lax.dynamic_update_slice_in_dim(empty_full, grad_acc[1], kv_slot, 1)]
    all_gather x1 -> x0, blocking collectives: 7.36 us -> none  [shards(): segs_all = lax.all_gather(seg_ids, 'inner', axis=0, tiled=True)]
    reduce_sum x2 -> x0, other arithmetic: 5.01 us -> none  [the longest x1 2.79 us: shards(): jnp.sum(jnp.exp(block - row_max[..., None]), -1)]
  transfers between devices with their start and end apart: 11 -> 0, of which waited for: 4 -> 0; matrix products, arithmetic and copies ran while one was open for 32% -> 0% of each run, Pallas kernels for 0% -> 0%
where the time goes in v1:
time: 57.6 us; the launch traced here: 57.4 us
  Pallas kernels  47.8 us (83%)
  local copies, waits for them, and re-layouts  8.81 us (15%)
  between operations  0.74 us (1%)
    pallas_call x1, Pallas kernels, shards(): pl.pallas_call(functools.partial(kernel, (n_in, reach, n_out, kvl, gh, sh...  47.8 us
    unnamed x10, local copies, waits for them, and re-layouts  3.08 us
    reshape x2, local copies, waits for them, and re-layouts, ungrouped(): x.reshape(kvl, tok, gh, depth).transpose(1, 0, 2, 3)  2.3 us
    broadcast_in_dim x3, local copies, waits for them, and re-layouts, shards(): seg_q = jnp.broadcast_to(jnp.repeat(seg_ids, gh)[:, None], (rows, tok // 2))  1.5 us
    dynamic_slice x1, local copies, waits for them, and re-layouts, shards(): lax.dynamic_slice_in_dim(x, slot, kvl, 1).transpose(1, 0, 2)  1.48 us

profile of v1, /device:TPU:1, one launch (start us, length us, event | category | flops | bytes accessed | tf_op | source)
XLA Modules:
  0.0 57.4 jit_solution(16648902780263282855)
XLA Ops:
  0.6 0.0 copy-start
  0.7 0.0 copy-start.2
  0.7 0.8 %copy-done.2 = s32[256]{0:T(256)S(1)} copy-done((s32[256]{0:T(256)S(1)}, s32[256]{0:T(256)}, u32[]{:S(2)}) %copy-start.2) | copy-done | bytes 1048
  1.4 0.1 broadcast_in_dim.17
  1.5 0.1 broadcast_in_dim.18
  1.6 1.5 %constant_dynamic-slice_fusion = (bf16[256,2,128]{2,1,0:T(2,128)(2,1)S(1)}, bf16[256,2,128]{2,1,0:T(2,128)(2,1)S(1)}) fusion(bf16[256,8,128]{2,1,0:T(8,128)(2,1)} %param.7, s32[]{:T(128)S(6)} %select_n.10, bf16[256,8,128]{2,1,0:T(8,128)(2,1)} %param.6), kind=kLoop, calls=%fused_computation.9 | loop fusion | bytes 524292 | tf_op jit(solution)/shard_map/dynamic_slice | solution.py:347
  3.1 0.0 copy-start.1
  3.2 1.3 %broadcast_in_dim.19.segq_ref = s32[2048,128]{1,0:T(8,128)} broadcast(s32[2048]{0:T(1024)S(1)} %broadcast_in_dim.18), dimensions={0} | broadcast | bytes 1056768 | tf_op jit(solution)/shard_map/broadcast_in_dim | solution.py:350
  4.5 0.0 copy-done
  4.5 0.0 copy-done.1
  4.5 0.4 copy_bitcast_fusion.2
  4.9 47.8 %shard_map.84 = (bf16[2,2048,128]{2,1,0:T(8,128)(2,1)S(1)}, bf16[2,2048,128]{2,1,0:T(8,128)(2,1)S(1)}, bf16[8,2,256,128]{3,2,1,0:T(8,128)(2,1)S(1)}) custom-call(bf16[2,2048,128]{2,1,0:T(8,128)(2,1)S(1)} %get-tuple-element.23.q_ref, bf16[2,2048,128]{2,1,0:T(8,128)(2,1)S(1)} %get-tuple-element.22.do_ref, bf16[2,2,256,128]{3,2,1,0:T(8,128)(2,1)S(1)} %pad_maximum_fusion.kv_ref, ...), custom_call_target="tpu_custom_call" | custom-call | tf_op jit(solution)/shard_map/pallas_call | solution.py:354
  52.7 1.2 %copy_bitcast_fusion.1 = bf16[256,16,128]{2,1,0:T(8,128)(2,1)} fusion(bf16[2,2048,128]{2,1,0:T(8,128)(2,1)S(1)} %get-tuple-element.7), kind=kLoop, calls=%fused_computation.1 | loop fusion | bytes 2097152 | tf_op jit(solution)/shard_map/reshape | solution.py:344
  53.8 1.1 %copy_bitcast_fusion = bf16[256,16,128]{2,1,0:T(8,128)(2,1)} fusion(bf16[2,2048,128]{2,1,0:T(8,128)(2,1)S(1)} %get-tuple-element.8), kind=kLoop, calls=%fused_computation | loop fusion | bytes 2097152 | tf_op jit(solution)/shard_map/reshape | solution.py:344
  55.0 0.1 slice_bitcast_fusion
  55.1 1.1 %copy.24 = bf16[256,8,128]{2,1,0:T(8,128)(2,1)} copy(bf16[256,8,128]{2,0,1:T(8,128)(2,1)S(1)} %get-tuple-element.18) | data formatting | bytes 1048576
  56.2 1.1 %copy.23 = bf16[256,8,128]{2,1,0:T(8,128)(2,1)} copy(bf16[256,8,128]{2,0,1:T(8,128)(2,1)S(1)} %get-tuple-element.19) | data formatting | bytes 1048576
  (4 shorter events, 0.1 us)
Async XLA Ops:
  0.6 3.9 %copy-start = (bf16[256,16,128]{2,1,0:T(8,128)(2,1)S(1)}, bf16[256,16,128]{2,1,0:T(8,128)(2,1)}, u32[]{:S(2)}) copy-start(bf16[256,16,128]{2,1,0:T(8,128)(2,1)} %param.5) | copy-start | bytes 3145732
  0.7 0.8 %copy-start.2 = (s32[256]{0:T(256)S(1)}, s32[256]{0:T(256)}, u32[]{:S(2)}) copy-start(s32[256]{0:T(256)} %param.9) | copy-start | bytes 3076
  3.1 1.4 %copy-start.1 = (bf16[256,16,128]{2,1,0:T(8,128)(2,1)S(1)}, bf16[256,16,128]{2,1,0:T(8,128)(2,1)}, u32[]{:S(2)}) copy-start(bf16[256,16,128]{2,1,0:T(8,128)(2,1)} %param.8) | copy-start | bytes 3145732

commit v2 on v1

--- a/solution.py
+++ b/solution.py
@@ -20,9 +20,9 @@
 
 
 def kernel(
-    cfg, q_ref, do_ref, kv_ref, segrow_ref, segq_ref,
+    cfg, q_ref, do_ref, key_ref, value_ref, segrow_ref,
     out_ref, dq_ref, grads_ref,
-    kv_buf, seg_buf, kcat, vcat, segcat, p_buf, ds_buf, dkcat, dvcat,
+    kv_ref, segq_ref, flat, kv_buf, seg_buf, kcat, vcat, segcat, p_buf, ds_buf, dkcat, dvcat,
     back_send, back_recv, gather, share_recv,
     kv_ssem, kv_rsem, seg_ssem, seg_rsem, b_ssem, b_rsem, g_ssem, g_rsem, h_ssem, h_rsem,
 ):
@@ -34,6 +34,12 @@
     pos = lax.axis_index("inner")
     outer = lax.axis_index("outer")
     core = lax.axis_index("heads")
+    slot = (outer * 2 + core) * kvl // share
+
+    for c, ref in ((0, key_ref), (1, value_ref)):
+        flat[...] = ref[...].astype(jnp.float32).reshape(flat.shape)
+        for g in range(kvl):
+            kv_ref[g, c] = flat[pl.ds(slot + g, tok, stride=ref.shape[1]), :].astype(kv_ref.dtype)
 
     barrier = pltpu.get_barrier_semaphore()
 
@@ -53,11 +59,11 @@
     ends = jnp.where(pos > 0, 1, 0) + jnp.where(pos < n_in - 1, 1, 0)
     pl.semaphore_wait(barrier, ends + n_out)
 
-    def kv_copy(g, d):
-        src = kv_ref.at[g] if d == 1 else kv_buf.at[g, d - 2]
-        return pltpu.make_async_remote_copy(
-            src_ref=src, dst_ref=kv_buf.at[g, d - 1],
-            send_sem=kv_ssem.at[g, d - 1], recv_sem=kv_rsem.at[g, d - 1],
+    def kv_copy(g, c, d):
+        src = kv_ref.at[g, c] if d == 1 else kv_buf.at[g, d - 2, c]
+        return pltpu.make_async_remote_copy(
+            src_ref=src, dst_ref=kv_buf.at[g, d - 1, c],
+            send_sem=kv_ssem.at[g, d - 1, c], recv_sem=kv_rsem.at[g, d - 1, c],
             device_id={"inner": pos + 1}, device_id_type=MESH,
         )
 
@@ -75,12 +81,34 @@
     def back_receives(d):
         return (pos + 1 < n_in) & (pos + 1 >= d)
 
-    def start_hop(d):
-        @pl.when(sends(d))
-        def _():
-            seg_copy(d).start()
-            for g in range(kvl):
-                kv_copy(g, d).start()
+    def start_own(g):
+        @pl.when(sends(1))
+        def _():
+            for c in range(2):
+                kv_copy(g, c, 1).start()
+
+    def forward(g):
+        for d in range(1, reach):
+            for c in range(2):
+                @pl.when(pos >= d)
+                def _():
+                    kv_copy(g, c, d).wait_recv()
+
+                @pl.when(sends(d + 1))
+                def _():
+                    kv_copy(g, c, d + 1).start()
+
+    def farthest(g):
+        @pl.when(pos >= reach)
+        def _():
+            for c in range(2):
+                kv_copy(g, c, reach).wait_recv()
+
+    start_own(0)
+
+    @pl.when(sends(1))
+    def _():
+        seg_copy(1).start()
 
     for d in range(1, reach + 1):
         @pl.when(pos < d)
@@ -94,25 +122,22 @@
             for g in range(kvl):
                 back_recv[g, d - 1] = jnp.zeros(back_recv.shape[2:], back_recv.dtype)
 
-    start_hop(1)
+    seg_col = jnp.transpose(jnp.broadcast_to(segrow_ref[0:1, :], (half, tok)))
+    for j in range(gh):
+        segq_ref[pl.ds(j, tok, stride=gh), :] = seg_col
     for d in range(1, reach + 1):
         @pl.when(pos >= d)
         def _():
             seg_copy(d).wait_recv()
-            kv_copy(0, d).wait_recv()
+
         if d < reach:
             @pl.when(sends(d + 1))
             def _():
                 seg_copy(d + 1).start()
-                kv_copy(0, d + 1).start()
-            for g in range(1, kvl):
-                @pl.when(pos >= d)
-                def _():
-                    kv_copy(g, d).wait_recv()
-
-                @pl.when(sends(d + 1))
-                def _():
-                    kv_copy(g, d + 1).start()
+    forward(0)
+    for g in range(1, kvl):
+        start_own(g)
+    farthest(0)
 
     def block(g, c, d, rows):
         if d == 0:
@@ -193,9 +218,13 @@
             return carry
 
         lax.fori_loop(0, chunks, chunk, 0)
+
+    def weigh(g, hf, c):
         where = pl.ds(hf * rows_half, rows_half)
-        dkcat[g, hf] = dot(ds_buf[...], q_ref[g, where, :], 0, 0)
-        dvcat[g, hf] = dot(p_buf[...], do_ref[g, where, :], 0, 0)
+        if c == 0:
+            dkcat[g, hf] = dot(ds_buf[...], q_ref[g, where, :], 0, 0)
+        else:
+            dvcat[g, hf] = dot(p_buf[...], do_ref[g, where, :], 0, 0)
 
     def partial(g, c, d, part):
         cat = (dkcat if c == 0 else dvcat).at[g]
@@ -210,99 +239,108 @@
         at = tok + half + (d - 1) * tok + part * half
         return cat[0, at:at + half, :] + cat[1, at:at + half, :]
 
-    def back_copy(g, d):
-        return pltpu.make_async_remote_copy(
-            src_ref=back_send.at[g, d - 1], dst_ref=back_recv.at[g, d - 1],
-            send_sem=b_ssem.at[g, d - 1], recv_sem=b_rsem.at[g, d - 1],
+    def back_copy(g, d, c, part):
+        at = (g, d - 1, c, mixes[part])
+        return pltpu.make_async_remote_copy(
+            src_ref=back_send.at[at], dst_ref=back_recv.at[at],
+            send_sem=b_ssem.at[g, d - 1, c, part], recv_sem=b_rsem.at[g, d - 1, c, part],
             device_id={"inner": pos - 1}, device_id_type=MESH,
         )
 
-    def summed(ref, g, d):
-        for c in range(2):
-            for part in range(2):
-                term = partial(g, c, d, part)
-                if d < reach:
-                    term = term + back_recv[g, d, c, mixes[part], :].astype(jnp.float32)
-                ref[c, mixes[part], :] = term.astype(ref.dtype)
-
-    slot = (outer * 2 + core) * kvl // share
-
-    def final(g):
-        return gather.at[slot + g]
-
-    def outer_copy(g, o):
-        return pltpu.make_async_remote_copy(
-            src_ref=final(g), dst_ref=final(g),
-            send_sem=g_ssem.at[g, o - 1], recv_sem=g_rsem.at[g, o - 1],
+    def summed(g, d, c, part):
+        term = partial(g, c, d, part)
+        if d < reach:
+            term = term + back_recv[g, d, c, mixes[part], :].astype(jnp.float32)
+        return term
+
+    def outer_copy(g, o, c, part):
+        at = gather.at[slot + g, c, mixes[part]]
+        return pltpu.make_async_remote_copy(
+            src_ref=at, dst_ref=at,
+            send_sem=g_ssem.at[g, o - 1, c, part], recv_sem=g_rsem.at[g, o - 1, c, part],
             device_id={"outer": lax.rem(outer + o, n_out)}, device_id_type=MESH,
         )
 
-    def sibling_copy(g, o):
+    def sibling_copy(g, o, c, part):
         src_outer = lax.rem(outer - o + n_out, n_out)
-        at = gather.at[(src_outer * 2 + core) * kvl // share + g]
+        at = gather.at[(src_outer * 2 + core) * kvl // share + g, c, mixes[part]]
         return pltpu.make_async_remote_copy(
             src_ref=at, dst_ref=at,
-            send_sem=h_ssem.at[g, o], recv_sem=h_rsem.at[g, o],
+            send_sem=h_ssem.at[g, o, c, part], recv_sem=h_rsem.at[g, o, c, part],
             device_id={"heads": 1 - core}, device_id_type=MESH,
         )
 
-    def share_copy(g):
-        return pltpu.make_async_remote_copy(
-            src_ref=final(g), dst_ref=share_recv.at[g],
-            send_sem=h_ssem.at[g, 0], recv_sem=h_rsem.at[g, 0],
+    def share_copy(g, c, part):
+        return pltpu.make_async_remote_copy(
+            src_ref=gather.at[slot + g, c, mixes[part]], dst_ref=share_recv.at[g, c, mixes[part]],
+            send_sem=h_ssem.at[g, 0, c, part], recv_sem=h_rsem.at[g, 0, c, part],
             device_id={"heads": 1 - core}, device_id_type=MESH,
         )
 
-    def chain_step(g, d):
+    pieces = [(c, part) for c in (1, 0) for part in (0, 1)]
+
+    def step(g, d, c, part):
         if d < reach:
             @pl.when(back_receives(d + 1))
             def _():
-                back_copy(g, d + 1).wait_recv()
+                back_copy(g, d + 1, c, part).wait_recv()
         if d > 0:
-            summed(back_send.at[g, d - 1], g, d)
+            back_send[g, d - 1, c, mixes[part], :] = summed(g, d, c, part).astype(back_send.dtype)
 
             @pl.when(pos >= d)
             def _():
-                back_copy(g, d).start()
+                back_copy(g, d, c, part).start()
             return
-        summed(final(g), g, 0)
+        own = gather.at[slot + g, c, mixes[part]]
+        own[...] = summed(g, 0, c, part).astype(gather.dtype)
         if share > 1:
-            copy = share_copy(g)
+            copy = share_copy(g, c, part)
             copy.start()
             copy.wait()
-            final(g)[...] = (
-                final(g)[...].astype(jnp.float32) + share_recv[g].astype(jnp.float32)
-            ).astype(gather.dtype)
-        else:
-            sibling_copy(g, 0).start()
+            got = share_recv[g, c, mixes[part], :].astype(jnp.float32)
+            own[...] = (own[...].astype(jnp.float32) + got).astype(gather.dtype)
         for o in range(1, n_out):
-            outer_copy(g, o).start()
+            outer_copy(g, o, c, part).start()
+        if share == 1:
+            sibling_copy(g, 0, c, part).start()
+
+    def arrive(g):
+        for c, part in pieces:
+            for o in range(1, n_out):
+                outer_copy(g, o, c, part).wait_recv()
+                if share == 1:
+                    sibling_copy(g, o, c, part).start()
 
     for g in range(kvl):
         if g > 0:
-            @pl.when(pos >= reach)
-            def _():
-                kv_copy(g, reach).wait_recv()
-        for hf in range(2):
-            compute(g, hf)
-            if g > 0 and hf == 0:
-                for d in range(reach - 1, 0, -1):
-                    chain_step(g - 1, d)
+            farthest(g)
+        compute(g, 0)
+        for c in (1, 0):
+            weigh(g, 0, c)
+            step(g, reach, c, 0)
+        if g + 1 < kvl:
+            forward(g + 1)
         if g > 0:
-            chain_step(g - 1, 0)
-        chain_step(g, reach)
+            for d in range(reach - 1, 0, -1):
+                for c, part in pieces:
+                    step(g - 1, d, c, part)
+        compute(g, 1)
+        for c in (1, 0):
+            weigh(g, 1, c)
+            step(g, reach, c, 1)
+        if g > 0:
+            for c, part in pieces:
+                step(g - 1, 0, c, part)
     for d in range(reach - 1, -1, -1):
-        chain_step(kvl - 1, d)
-
+        for c, part in pieces:
+            step(kvl - 1, d, c, part)
     for g in range(kvl):
-        for o in range(1, n_out):
-            outer_copy(g, o).wait_recv()
-            if share == 1:
-                sibling_copy(g, o).start()
+        arrive(g)
     if share == 1:
         for g in range(kvl):
-            for o in range(n_out):
-                sibling_copy(g, o).wait_recv()
+            for c, part in pieces:
+                for o in range(n_out):
+                    sibling_copy(g, o, c, part).wait_recv()
     grads_ref[...] = gather[...]
 
     for d in range(1, reach + 1):
@@ -310,18 +348,21 @@
         def _():
             seg_copy(d).wait_send()
             for g in range(kvl):
-                kv_copy(g, d).wait_send()
+                for c in range(2):
+                    kv_copy(g, c, d).wait_send()
 
         @pl.when(pos >= d)
         def _():
             for g in range(kvl):
-                back_copy(g, d).wait_send()
+                for c, part in pieces:
+                    back_copy(g, d, c, part).wait_send()
     for g in range(kvl):
-        for o in range(1, n_out):
-            outer_copy(g, o).wait_send()
-        if share == 1:
-            for o in range(n_out):
-                sibling_copy(g, o).wait_send()
+        for c, part in pieces:
+            for o in range(1, n_out):
+                outer_copy(g, o, c, part).wait_send()
+            if share == 1:
+                for o in range(n_out):
+                    sibling_copy(g, o, c, part).wait_send()
 
 
 def shards(queries, keys, values, grad_out, seg_ids):
@@ -334,7 +375,6 @@
     reach = n_in // 2
     rows = tok * gh
     width = tok + (tok // 2) + tok * (reach - 1)
-    slot = lax.axis_index(("outer", "heads")) * heads // GROUP
     wire = jnp.bfloat16 if reach <= 2 else jnp.float32
 
     def grouped(x):
@@ -343,11 +383,7 @@
     def ungrouped(x):
         return x.reshape(kvl, tok, gh, depth).transpose(1, 0, 2, 3).reshape(tok, heads, depth)
 
-    kv_own = jnp.stack(
-        [lax.dynamic_slice_in_dim(x, slot, kvl, 1).transpose(1, 0, 2) for x in (keys, values)], 1
-    )
     seg_row = jnp.broadcast_to(seg_ids[None, :], (8, tok))
-    seg_q = jnp.broadcast_to(jnp.repeat(seg_ids, gh)[:, None], (rows, tok // 2))
     bf, f32 = jnp.bfloat16, jnp.float32
     dma = pltpu.SemaphoreType.DMA
     vmem = pl.BlockSpec(memory_space=pltpu.VMEM)
@@ -361,6 +397,9 @@
         in_specs=[vmem] * 5,
         out_specs=(vmem,) * 3,
         scratch_shapes=[
+            pltpu.VMEM((kvl, 2, tok, depth), bf),
+            pltpu.VMEM((rows, tok // 2), jnp.int32),
+            pltpu.VMEM((tok * kv_total, depth), f32),
             pltpu.VMEM((kvl, reach, 2, tok, depth), bf),
             pltpu.VMEM((reach, 8, tok), jnp.int32),
             pltpu.VMEM((width, depth), bf),
@@ -374,16 +413,16 @@
             pltpu.VMEM((kvl, reach, 2, tok, depth), wire),
             pltpu.VMEM((kv_total, 2, tok, depth), bf),
             pltpu.VMEM((kvl, 2, tok, depth), bf),
-            dma((kvl, reach)), dma((kvl, reach)),
+            dma((kvl, reach, 2)), dma((kvl, reach, 2)),
             dma((reach,)), dma((reach,)),
-            dma((kvl, reach)), dma((kvl, reach)),
-            dma((kvl, n_out)), dma((kvl, n_out)),
-            dma((kvl, n_out)), dma((kvl, n_out)),
+            dma((kvl, reach, 2, 2)), dma((kvl, reach, 2, 2)),
+            dma((kvl, n_out, 2, 2)), dma((kvl, n_out, 2, 2)),
+            dma((kvl, n_out, 2, 2)), dma((kvl, n_out, 2, 2)),
         ],
         compiler_params=pltpu.CompilerParams(
             collective_id=0, has_side_effects=True, vmem_limit_bytes=48 * 2**20
         ),
-    )(grouped(queries), grouped(grad_out), kv_own, seg_row, seg_q)
+    )(grouped(queries), grouped(grad_out), keys, values, seg_row)
     return (
         ungrouped(out),
         ungrouped(dq),

time: 57.6 us -> 54.3 us (0.943)
  Pallas kernels: 47.8 us -> 44.9 us
    pallas_call x1, Pallas kernels: 47.8 us -> 44.9 us  [shards(): pl.pallas_call(functools.partial(kernel, (n_in, reach, n_out, kvl, gh, sh...]
    reshape x1, local copies, waits for them, and re-layouts: 0.36 us -> 2.64 us  [grouped(): x.reshape(tok, kvl, gh, depth).transpose(1, 0, 2, 3)]
    broadcast_in_dim x3 -> x0, local copies, waits for them, and re-layouts: 1.5 us -> none  [shards(): seg_q = jnp.broadcast_to(jnp.repeat(seg_ids, gh)[:, None], (rows, tok // 2))]
    dynamic_slice x1 -> x0, local copies, waits for them, and re-layouts: 1.48 us -> none  [shards(): lax.dynamic_slice_in_dim(x, slot, kvl, 1).transpose(1, 0, 2)]
    broadcast_in_dim x1, local copies, waits for them, and re-layouts: 0.01 us -> 0.77 us  [shards(): seg_row = jnp.broadcast_to(seg_ids[None, :], (8, tok))]
    unnamed x10 -> x8, local copies, waits for them, and re-layouts: 3.08 us -> 2.75 us
where the time goes in v2:
time: 54.3 us; the launch traced here: 54.1 us
  Pallas kernels  44.9 us (83%)
  local copies, waits for them, and re-layouts  8.55 us (16%)
  between operations  0.66 us (1%)
    pallas_call x1, Pallas kernels, shards(): pl.pallas_call(functools.partial(kernel, (n_in, reach, n_out, kvl, gh, sh...  44.9 us
    unnamed x8, local copies, waits for them, and re-layouts  2.75 us
    reshape x1, local copies, waits for them, and re-layouts, grouped(): x.reshape(tok, kvl, gh, depth).transpose(1, 0, 2, 3)  2.64 us
    reshape x2, local copies, waits for them, and re-layouts, ungrouped(): x.reshape(kvl, tok, gh, depth).transpose(1, 0, 2, 3)  2.3 us

profile of v2, /device:TPU:1, one launch (start us, length us, event | category | flops | bytes accessed | tf_op | source)
XLA Modules:
  0.0 54.1 jit_solution(1620109235387152099)
XLA Ops:
  0.6 0.0 copy-start
  0.6 0.8 %broadcast_in_dim.2.segrow_ref = s32[8,256]{1,0:T(8,128)S(1)} broadcast(s32[256]{0:T(256)} %param.9), dimensions={1} | broadcast | bytes 9216 | tf_op jit(solution)/shard_map/broadcast_in_dim | solution.py:386
  1.4 0.5 copy-done
  1.9 0.0 copy-start.1
  1.9 0.0 copy-start.2
  1.9 2.6 %copy_bitcast_fusion.2 = (bf16[2,2048,128]{2,1,0:T(8,128)(2,1)}, bf16[2,2048,128]{2,1,0:T(8,128)(2,1)S(1)}) fusion(bf16[256,16,128]{2,1,0:T(8,128)(2,1)S(1)} %copy-done, bf16[256,16,128]{2,1,0:T(8,128)(2,1)} %param.8), kind=kLoop, calls=%fused_computation.2 | loop fusion | bytes 4194304 | tf_op jit(solution)/shard_map/reshape | solution.py:381
  4.5 0.0 copy-done.1
  4.5 0.0 copy-done.2
  4.5 44.9 %shard_map.84 = (bf16[2,2048,128]{2,1,0:T(8,128)(2,1)S(1)}, bf16[2,2048,128]{2,1,0:T(8,128)(2,1)S(1)}, bf16[8,2,256,128]{3,2,1,0:T(8,128)(2,1)S(1)}) custom-call(bf16[2,2048,128]{2,1,0:T(8,128)(2,1)S(1)} %get-tuple-element.17.q_ref, bf16[2,2048,128]{2,1,0:T(8,128)(2,1)} %get-tuple-element.16.do_ref, bf16[256,8,128]{2,1,0:T(8,128)(2,1)S(1)} %copy-done.1, ...), custom_call_target="tpu_custom_call" | custom-call | tf_op jit(solution)/shard_map/pallas_call | solution.py:390
  49.5 1.2 %copy_bitcast_fusion.1 = bf16[256,16,128]{2,1,0:T(8,128)(2,1)} fusion(bf16[2,2048,128]{2,1,0:T(8,128)(2,1)S(1)} %get-tuple-element.7), kind=kLoop, calls=%fused_computation.1 | loop fusion | bytes 2097152 | tf_op jit(solution)/shard_map/reshape | solution.py:384
  50.6 1.1 %copy_bitcast_fusion = bf16[256,16,128]{2,1,0:T(8,128)(2,1)} fusion(bf16[2,2048,128]{2,1,0:T(8,128)(2,1)S(1)} %get-tuple-element.8), kind=kLoop, calls=%fused_computation | loop fusion | bytes 2097152 | tf_op jit(solution)/shard_map/reshape | solution.py:384
  51.8 0.1 slice_bitcast_fusion
  51.9 1.1 %copy.14 = bf16[256,8,128]{2,1,0:T(8,128)(2,1)} copy(bf16[256,8,128]{2,0,1:T(8,128)(2,1)S(1)} %get-tuple-element.14) | data formatting | bytes 1048576
  53.0 1.1 %copy.13 = bf16[256,8,128]{2,1,0:T(8,128)(2,1)} copy(bf16[256,8,128]{2,0,1:T(8,128)(2,1)S(1)} %get-tuple-element.15) | data formatting | bytes 1048576
Async XLA Ops:
  0.6 1.2 %copy-start = (bf16[256,16,128]{2,1,0:T(8,128)(2,1)S(1)}, bf16[256,16,128]{2,1,0:T(8,128)(2,1)}, u32[]{:S(2)}) copy-start(bf16[256,16,128]{2,1,0:T(8,128)(2,1)} %param.5) | copy-start | bytes 3145732
  1.9 2.6 %copy-start.1 = (bf16[256,8,128]{2,1,0:T(8,128)(2,1)S(1)}, bf16[256,8,128]{2,1,0:T(8,128)(2,1)}, u32[]{:S(2)}) copy-start(bf16[256,8,128]{2,1,0:T(8,128)(2,1)} %key_ref.1) | copy-start | bytes 1572868
  1.9 2.6 %copy-start.2 = (bf16[256,8,128]{2,1,0:T(8,128)(2,1)S(1)}, bf16[256,8,128]{2,1,0:T(8,128)(2,1)}, u32[]{:S(2)}) copy-start(bf16[256,8,128]{2,1,0:T(8,128)(2,1)} %value_ref.1) | copy-start | bytes 1572868

commit v3 on v2

--- a/solution.py
+++ b/solution.py
@@ -20,15 +20,16 @@
 
 
 def kernel(
-    cfg, q_ref, do_ref, key_ref, value_ref, segrow_ref,
-    out_ref, dq_ref, grads_ref,
-    kv_ref, segq_ref, flat, kv_buf, seg_buf, kcat, vcat, segcat, p_buf, ds_buf, dkcat, dvcat,
+    cfg, q_arg, do_arg, key_ref, value_ref, seg_arg,
+    out_res, dq_res, dk_res, dv_res,
+    q_in, do_in, q_ref, do_ref, out_ref, dq_ref, segrow_ref, in_sem, kv_ref, segq_ref, flat, kv_buf, seg_buf, kcat, vcat, segcat, p_buf, ds_buf, dkcat, dvcat,
     back_send, back_recv, gather, share_recv,
     kv_ssem, kv_rsem, seg_ssem, seg_rsem, b_ssem, b_rsem, g_ssem, g_rsem, h_ssem, h_rsem,
 ):
     n_in, reach, n_out, kvl, gh, share, tok = cfg
     head_dim = q_ref.shape[-1]
     half = tok // 2
+    native = gh % 8 == 0
     scale = head_dim ** (-0.5)
     width = half + half + tok * (reach - 1)
     pos = lax.axis_index("inner")
@@ -36,10 +37,17 @@
     core = lax.axis_index("heads")
     slot = (outer * 2 + core) * kvl // share
 
+    loads = [
+        pltpu.make_async_copy(arg, buf, in_sem.at[i])
+        for i, (arg, buf) in enumerate(((q_arg, q_in), (do_arg, do_in)))
+    ]
+    for load in loads:
+        load.start()
+    segrow_ref[...] = jnp.broadcast_to(seg_arg[...], segrow_ref.shape)
     for c, ref in ((0, key_ref), (1, value_ref)):
-        flat[...] = ref[...].astype(jnp.float32).reshape(flat.shape)
+        flat[c] = ref[...].astype(jnp.float32).reshape(flat.shape[1:])
         for g in range(kvl):
-            kv_ref[g, c] = flat[pl.ds(slot + g, tok, stride=ref.shape[1]), :].astype(kv_ref.dtype)
+            kv_ref[g, c] = flat[c, pl.ds(slot + g, tok, stride=ref.shape[1]), :].astype(kv_ref.dtype)
 
     barrier = pltpu.get_barrier_semaphore()
 
@@ -122,9 +130,6 @@
             for g in range(kvl):
                 back_recv[g, d - 1] = jnp.zeros(back_recv.shape[2:], back_recv.dtype)
 
-    seg_col = jnp.transpose(jnp.broadcast_to(segrow_ref[0:1, :], (half, tok)))
-    for j in range(gh):
-        segq_ref[pl.ds(j, tok, stride=gh), :] = seg_col
     for d in range(1, reach + 1):
         @pl.when(pos >= d)
         def _():
@@ -135,8 +140,25 @@
             def _():
                 seg_copy(d + 1).start()
     forward(0)
-    for g in range(1, kvl):
-        start_own(g)
+    seg_col = jnp.transpose(jnp.broadcast_to(segrow_ref[0:1, :], (half, tok)))
+    for j in range(gh):
+        segq_ref[pl.ds(j, tok, stride=gh), :] = seg_col
+    for load, buf, ref in zip(loads, (q_in, do_in), (q_ref, do_ref)):
+        load.wait()
+        for g in range(kvl):
+            if native:
+                wide = buf[:, g * gh:(g + 1) * gh, :].astype(jnp.float32)
+                ref[g] = wide.reshape(tok * gh, head_dim).astype(ref.dtype)
+            else:
+                ref[g] = buf[g]
+    if kvl > 1:
+        @pl.when(sends(reach))
+        def _():
+            for c in range(2):
+                kv_copy(0, c, reach).wait_send()
+
+        for g in range(1, kvl):
+            start_own(g)
     farthest(0)
 
     def block(g, c, d, rows):
@@ -277,7 +299,7 @@
             device_id={"heads": 1 - core}, device_id_type=MESH,
         )
 
-    pieces = [(c, part) for c in (1, 0) for part in (0, 1)]
+    pieces = [(c, part) for part in (0, 1) for c in (1, 0)]
 
     def step(g, d, c, part):
         if d < reach:
@@ -311,6 +333,7 @@
                 if share == 1:
                     sibling_copy(g, o, c, part).start()
 
+    early = reach > 1
     for g in range(kvl):
         if g > 0:
             farthest(g)
@@ -328,11 +351,23 @@
         for c in (1, 0):
             weigh(g, 1, c)
             step(g, reach, c, 1)
+            if early and g + 1 == kvl:
+                step(g, reach - 1, c, 0)
         if g > 0:
             for c, part in pieces:
                 step(g - 1, 0, c, part)
+    for buf, ref in ((out_ref, out_res), (dq_ref, dq_res)):
+        if native:
+            parts = [
+                buf[g].astype(jnp.float32).reshape(tok, gh, head_dim) for g in range(kvl)
+            ]
+            ref[...] = jnp.concatenate(parts, 1).astype(ref.dtype)
+        else:
+            ref[...] = buf[...]
     for d in range(reach - 1, -1, -1):
         for c, part in pieces:
+            if early and d == reach - 1 and part == 0:
+                continue
             step(kvl - 1, d, c, part)
     for g in range(kvl):
         arrive(g)
@@ -341,7 +376,11 @@
             for c, part in pieces:
                 for o in range(n_out):
                     sibling_copy(g, o, c, part).wait_recv()
-    grads_ref[...] = gather[...]
+    kv_total = gather.shape[0]
+    for c, ref in ((0, dk_res), (1, dv_res)):
+        for k in range(kv_total):
+            flat[c, pl.ds(k, tok, stride=kv_total), :] = gather[k, c].astype(jnp.float32)
+        ref[...] = flat[c].reshape(ref.shape).astype(ref.dtype)
 
     for d in range(1, reach + 1):
         @pl.when(sends(d))
@@ -349,7 +388,8 @@
             seg_copy(d).wait_send()
             for g in range(kvl):
                 for c in range(2):
-                    kv_copy(g, c, d).wait_send()
+                    if kvl == 1 or g > 0 or d < reach:
+                        kv_copy(g, c, d).wait_send()
 
         @pl.when(pos >= d)
         def _():
@@ -383,23 +423,26 @@
     def ungrouped(x):
         return x.reshape(kvl, tok, gh, depth).transpose(1, 0, 2, 3).reshape(tok, heads, depth)
 
-    seg_row = jnp.broadcast_to(seg_ids[None, :], (8, tok))
     bf, f32 = jnp.bfloat16, jnp.float32
     dma = pltpu.SemaphoreType.DMA
     vmem = pl.BlockSpec(memory_space=pltpu.VMEM)
-    out, dq, grads = pl.pallas_call(
+    acts = (tok, heads, depth) if gh % 8 == 0 else (kvl, rows, depth)
+    held = pltpu.VMEM((kvl, rows, depth), bf)
+    if gh % 8:
+        queries, grad_out = grouped(queries), grouped(grad_out)
+    out, dq, dk, dv = pl.pallas_call(
         functools.partial(kernel, (n_in, reach, n_out, kvl, gh, share, tok)),
-        out_shape=(
-            jax.ShapeDtypeStruct((kvl, rows, depth), bf),
-            jax.ShapeDtypeStruct((kvl, rows, depth), bf),
-            jax.ShapeDtypeStruct((kv_total, 2, tok, depth), bf),
+        out_shape=tuple(
+            jax.ShapeDtypeStruct(shape, bf) for shape in (acts, acts, keys.shape, keys.shape)
         ),
-        in_specs=[vmem] * 5,
-        out_specs=(vmem,) * 3,
+        in_specs=[pl.BlockSpec(memory_space=pl.ANY)] * 2 + [vmem] * 3,
+        out_specs=(vmem,) * 4,
         scratch_shapes=[
+            pltpu.VMEM(acts, bf), pltpu.VMEM(acts, bf), held, held, held, held,
+            pltpu.VMEM((8, tok), jnp.int32), dma((2,)),
             pltpu.VMEM((kvl, 2, tok, depth), bf),
             pltpu.VMEM((rows, tok // 2), jnp.int32),
-            pltpu.VMEM((tok * kv_total, depth), f32),
+            pltpu.VMEM((2, tok * kv_total, depth), f32),
             pltpu.VMEM((kvl, reach, 2, tok, depth), bf),
             pltpu.VMEM((reach, 8, tok), jnp.int32),
             pltpu.VMEM((width, depth), bf),
@@ -422,13 +465,10 @@
         compiler_params=pltpu.CompilerParams(
             collective_id=0, has_side_effects=True, vmem_limit_bytes=48 * 2**20
         ),
-    )(grouped(queries), grouped(grad_out), keys, values, seg_row)
-    return (
-        ungrouped(out),
-        ungrouped(dq),
-        grads[:, 0].transpose(1, 0, 2),
-        grads[:, 1].transpose(1, 0, 2),
-    )
+    )(queries, grad_out, keys, values, seg_ids[None, :])
+    if gh % 8:
+        out, dq = ungrouped(out), ungrouped(dq)
+    return out, dq, dk, dv
 
 
 def solution(mesh):

time: 54.3 us -> 53 us (0.976)
  local copies, waits for them, and re-layouts: 8.55 us -> 7.51 us
    reshape x3 -> x0, local copies, waits for them, and re-layouts: 4.94 us -> none  [the longest x1 2.64 us: grouped(): x.reshape(tok, kvl, gh, depth).transpose(1, 0, 2, 3)]
    unnamed x8 -> x12, local copies, waits for them, and re-layouts: 2.75 us -> 7.51 us
    broadcast_in_dim x1 -> x0, local copies, waits for them, and re-layouts: 0.77 us -> none  [shards(): seg_row = jnp.broadcast_to(seg_ids[None, :], (8, tok))]
where the time goes in v3:
time: 53 us; the launch traced here: 52.7 us
  Pallas kernels  44.6 us (84%)
  local copies, waits for them, and re-layouts  7.51 us (14%)
  between operations  0.65 us (1%)
    pallas_call x1, Pallas kernels, shards(): pl.pallas_call(functools.partial(kernel, (n_in, reach, n_out, kvl, gh, sh...  44.6 us
    unnamed x12, local copies, waits for them, and re-layouts  7.51 us

profile of v3, /device:TPU:1, one launch (start us, length us, event | category | flops | bytes accessed | tf_op | source)
XLA Modules:
  0.0 52.7 jit_solution(10012706674953478305)
XLA Ops:
  0.6 0.0 copy-start.3
  0.6 0.7 %copy-done.3 = s32[256]{0:T(256)S(1)} copy-done((s32[256]{0:T(256)S(1)}, s32[256]{0:T(256)}, u32[]{:S(2)}) %copy-start.3) | copy-done | bytes 1048
  1.3 0.0 copy-start
  1.3 1.2 %copy-done = bf16[256,16,128]{2,1,0:T(8,128)(2,1)S(1)} copy-done((bf16[256,16,128]{2,1,0:T(8,128)(2,1)S(1)}, bf16[256,16,128]{2,1,0:T(8,128)(2,1)}, u32[]{:S(2)}) %copy-start) | copy-done | bytes 1048600
  2.5 0.0 copy-start.1
  2.5 1.0 %copy-done.1 = bf16[256,8,128]{2,1,0:T(8,128)(2,1)S(1)} copy-done((bf16[256,8,128]{2,1,0:T(8,128)(2,1)S(1)}, bf16[256,8,128]{2,1,0:T(8,128)(2,1)}, u32[]{:S(2)}) %copy-start.1) | copy-done | bytes 524312
  3.6 0.0 copy-start.2
  3.6 1.0 %copy-done.2 = bf16[256,8,128]{2,1,0:T(8,128)(2,1)S(1)} copy-done((bf16[256,8,128]{2,1,0:T(8,128)(2,1)S(1)}, bf16[256,8,128]{2,1,0:T(8,128)(2,1)}, u32[]{:S(2)}) %copy-start.2) | copy-done | bytes 524312
  4.6 44.6 %shard_map.84 = (bf16[256,16,128]{2,1,0:T(8,128)(2,1)S(1)}, bf16[256,16,128]{2,1,0:T(8,128)(2,1)S(1)}, bf16[256,8,128]{2,1,0:T(8,128)(2,1)S(1)}, bf16[256,8,128]{2,1,0:T(8,128)(2,1)S(1)}) custom-call(bf16[256,16,128]{2,1,0:T(8,128)(2,1)S(1)} %copy-done, bf16[256,16,128]{2,1,0:T(8,128)(2,1)} %do_arg.1, bf16[256,8,128]{2,1,0:T(8,128)(2,1)S(1)} %copy-done.1, ...), custom_call_target="tpu_custom_call" | custom-call | tf_op jit(solution)/shard_map/pallas_call | solution.py:433
  49.2 1.0 %copy.13 = bf16[256,16,128]{2,1,0:T(8,128)(2,1)} copy(bf16[256,16,128]{2,1,0:T(8,128)(2,1)S(1)} %get-tuple-element.8) | data formatting | bytes 2097152
  50.2 1.0 %copy.14 = bf16[256,16,128]{2,1,0:T(8,128)(2,1)} copy(bf16[256,16,128]{2,1,0:T(8,128)(2,1)S(1)} %get-tuple-element.9) | data formatting | bytes 2097152
  51.1 0.8 %copy.15 = bf16[256,8,128]{2,1,0:T(8,128)(2,1)} copy(bf16[256,8,128]{2,1,0:T(8,128)(2,1)S(1)} %get-tuple-element.10) | data formatting | bytes 1048576
  51.9 0.8 %copy.16 = bf16[256,8,128]{2,1,0:T(8,128)(2,1)} copy(bf16[256,8,128]{2,1,0:T(8,128)(2,1)S(1)} %get-tuple-element.11) | data formatting | bytes 1048576
Async XLA Ops:
  0.6 0.7 %copy-start.3 = (s32[256]{0:T(256)S(1)}, s32[256]{0:T(256)}, u32[]{:S(2)}) copy-start(s32[256]{0:T(256)} %param.9) | copy-start | bytes 3076
  1.3 1.2 %copy-start = (bf16[256,16,128]{2,1,0:T(8,128)(2,1)S(1)}, bf16[256,16,128]{2,1,0:T(8,128)(2,1)}, u32[]{:S(2)}) copy-start(bf16[256,16,128]{2,1,0:T(8,128)(2,1)} %q_arg.1) | copy-start | bytes 3145732
  2.5 1.0 %copy-start.1 = (bf16[256,8,128]{2,1,0:T(8,128)(2,1)S(1)}, bf16[256,8,128]{2,1,0:T(8,128)(2,1)}, u32[]{:S(2)}) copy-start(bf16[256,8,128]{2,1,0:T(8,128)(2,1)} %key_ref.1) | copy-start | bytes 1572868
  3.6 1.0 %copy-start.2 = (bf16[256,8,128]{2,1,0:T(8,128)(2,1)S(1)}, bf16[256,8,128]{2,1,0:T(8,128)(2,1)}, u32[]{:S(2)}) copy-start(bf16[256,8,128]{2,1,0:T(8,128)(2,1)} %value_ref.1) | copy-start | bytes 1572868

commit v4 on v3

--- a/solution.py
+++ b/solution.py
@@ -182,7 +182,7 @@
             segcat[hf, :, at:at + tok] = seg_buf[d - 1]
 
     rows_half = half * gh
-    rows = min(512, rows_half)
+    rows = rows_half
     chunks = rows_half // rows
     tokens = rows // gh
 

time: 53 us -> 50.8 us (0.958)
  Pallas kernels: 44.6 us -> 42.4 us
    pallas_call x1, Pallas kernels: 44.6 us -> 42.4 us  [shards(): pl.pallas_call(functools.partial(kernel, (n_in, reach, n_out, kvl, gh, sh...]
where the time goes in v4:
time: 50.8 us; the launch traced here: 50.5 us
  Pallas kernels  42.4 us (83%)
  local copies, waits for them, and re-layouts  7.51 us (15%)
  between operations  0.65 us (1%)
    pallas_call x1, Pallas kernels, shards(): pl.pallas_call(functools.partial(kernel, (n_in, reach, n_out, kvl, gh, sh...  42.4 us
    unnamed x12, local copies, waits for them, and re-layouts  7.51 us

profile of v4, /device:TPU:1, one launch (start us, length us, event | category | flops | bytes accessed | tf_op | source)
XLA Modules:
  0.0 50.5 jit_solution(15150910158845331290)
XLA Ops:
  0.6 0.0 copy-start.3
  0.6 0.7 %copy-done.3 = s32[256]{0:T(256)S(1)} copy-done((s32[256]{0:T(256)S(1)}, s32[256]{0:T(256)}, u32[]{:S(2)}) %copy-start.3) | copy-done | bytes 1048
  1.3 0.0 copy-start
  1.3 1.2 %copy-done = bf16[256,16,128]{2,1,0:T(8,128)(2,1)S(1)} copy-done((bf16[256,16,128]{2,1,0:T(8,128)(2,1)S(1)}, bf16[256,16,128]{2,1,0:T(8,128)(2,1)}, u32[]{:S(2)}) %copy-start) | copy-done | bytes 1048600
  2.5 0.0 copy-start.1
  2.5 1.0 %copy-done.1 = bf16[256,8,128]{2,1,0:T(8,128)(2,1)S(1)} copy-done((bf16[256,8,128]{2,1,0:T(8,128)(2,1)S(1)}, bf16[256,8,128]{2,1,0:T(8,128)(2,1)}, u32[]{:S(2)}) %copy-start.1) | copy-done | bytes 524312
  3.6 0.0 copy-start.2
  3.6 1.0 %copy-done.2 = bf16[256,8,128]{2,1,0:T(8,128)(2,1)S(1)} copy-done((bf16[256,8,128]{2,1,0:T(8,128)(2,1)S(1)}, bf16[256,8,128]{2,1,0:T(8,128)(2,1)}, u32[]{:S(2)}) %copy-start.2) | copy-done | bytes 524312
  4.6 42.4 %shard_map.84 = (bf16[256,16,128]{2,1,0:T(8,128)(2,1)S(1)}, bf16[256,16,128]{2,1,0:T(8,128)(2,1)S(1)}, bf16[256,8,128]{2,1,0:T(8,128)(2,1)S(1)}, bf16[256,8,128]{2,1,0:T(8,128)(2,1)S(1)}) custom-call(bf16[256,16,128]{2,1,0:T(8,128)(2,1)S(1)} %copy-done, bf16[256,16,128]{2,1,0:T(8,128)(2,1)} %do_arg.1, bf16[256,8,128]{2,1,0:T(8,128)(2,1)S(1)} %copy-done.1, ...), custom_call_target="tpu_custom_call" | custom-call | tf_op jit(solution)/shard_map/pallas_call | solution.py:433
  47.0 1.0 %copy.13 = bf16[256,16,128]{2,1,0:T(8,128)(2,1)} copy(bf16[256,16,128]{2,1,0:T(8,128)(2,1)S(1)} %get-tuple-element.8) | data formatting | bytes 2097152
  48.0 1.0 %copy.14 = bf16[256,16,128]{2,1,0:T(8,128)(2,1)} copy(bf16[256,16,128]{2,1,0:T(8,128)(2,1)S(1)} %get-tuple-element.9) | data formatting | bytes 2097152
  48.9 0.8 %copy.15 = bf16[256,8,128]{2,1,0:T(8,128)(2,1)} copy(bf16[256,8,128]{2,1,0:T(8,128)(2,1)S(1)} %get-tuple-element.10) | data formatting | bytes 1048576
  49.7 0.8 %copy.16 = bf16[256,8,128]{2,1,0:T(8,128)(2,1)} copy(bf16[256,8,128]{2,1,0:T(8,128)(2,1)S(1)} %get-tuple-element.11) | data formatting | bytes 1048576
Async XLA Ops:
  0.6 0.7 %copy-start.3 = (s32[256]{0:T(256)S(1)}, s32[256]{0:T(256)}, u32[]{:S(2)}) copy-start(s32[256]{0:T(256)} %param.9) | copy-start | bytes 3076
  1.3 1.2 %copy-start = (bf16[256,16,128]{2,1,0:T(8,128)(2,1)S(1)}, bf16[256,16,128]{2,1,0:T(8,128)(2,1)}, u32[]{:S(2)}) copy-start(bf16[256,16,128]{2,1,0:T(8,128)(2,1)} %q_arg.1) | copy-start | bytes 3145732
  2.5 1.0 %copy-start.1 = (bf16[256,8,128]{2,1,0:T(8,128)(2,1)S(1)}, bf16[256,8,128]{2,1,0:T(8,128)(2,1)}, u32[]{:S(2)}) copy-start(bf16[256,8,128]{2,1,0:T(8,128)(2,1)} %key_ref.1) | copy-start | bytes 1572868
  3.6 1.0 %copy-start.2 = (bf16[256,8,128]{2,1,0:T(8,128)(2,1)S(1)}, bf16[256,8,128]{2,1,0:T(8,128)(2,1)}, u32[]{:S(2)}) copy-start(bf16[256,8,128]{2,1,0:T(8,128)(2,1)} %value_ref.1) | copy-start | bytes 1572868
